TPU v7x, 32 devices: a whole 2x2x4 slice. The times are simulated.
32 devices in a mesh: stream: 16 (over z, x, core), shard: 2 (over y).
Axes of the slice: x: 2, y: 2, z: 4, core: 2. Of those that a mesh axis runs over, the one named last changes fastest.
Arguments:
- tokens: bfloat16 [32, 768, 512], P(('stream', 'shard')), may hold values from -6 to 6
- memory: bfloat16 [32, 512, 512], P(('stream', 'shard')), may hold values from -6 to 6
- cmemory: bfloat16 [32, 512, 512], P(('stream', 'shard')), may hold values from -6 to 6
- doc_ids: int32 [32, 1792], P(('stream', 'shard')), may hold values from 0 to 7, never falling along the last dimension, each value on 1 to 448 neighbouring positions
- cotangent: bfloat16 [32, 768, 512], P(('stream', 'shard')), may hold values from -6 to 6
- qkv_weight: float32 [512, 1536], P('shard'), may hold values from -0.25 to 0.25
- out_weight: float32 [512, 512], P('shard'), may hold values from -2 to 2
- up_weight: float32 [512, 2048], P('shard'), may hold values from -0.25 to 0.25
- down_weight: float32 [2048, 512], P('shard'), may hold values from -0.125 to 0.125
- conv_weight: float32 [1536, 512], P('shard'), may hold values from -0.15625 to 0.15625
- norm_params: float32 [512, 4], P('shard'), may hold values from -0.6 to 1.4, as said below
- qkv_moment: float32 [512, 1536], P('shard'), may hold values from -48 to 48
- out_moment: float32 [512, 512], P('shard'), may hold values from -14 to 14
- up_moment: float32 [512, 2048], P('shard'), may hold values from -28 to 28
- down_moment: float32 [2048, 512], P('shard'), may hold values from -56 to 56
- norm_moment: float32 [512, 4], P('shard'), may hold values from -96 to 96
- qkv_average: float32 [512, 1536], P('shard'), may hold values from -0.25 to 0.25
- out_average: float32 [512, 512], P('shard'), may hold values from -2 to 2
- up_average: float32 [512, 2048], P('shard'), may hold values from -0.25 to 0.25
- down_average: float32 [2048, 512], P('shard'), may hold values from -0.125 to 0.125
- norm_average: float32 [512, 4], P('shard'), may hold values from -0.6 to 1.4, as said below
Outputs:
- output: bfloat16 [32, 768, 512], P(('stream', 'shard'))
- new_memory: bfloat16 [32, 512, 512], P(('stream', 'shard'))
- new_cmemory: bfloat16 [32, 512, 512], P(('stream', 'shard'))
- token_grad: bfloat16 [32, 768, 512], P(('stream', 'shard'))
- qkv_grad: float32 [512, 1536], P('shard')
- out_grad: float32 [512, 512], P('shard')
- up_grad: float32 [512, 2048], P('shard')
- down_grad: float32 [2048, 512], P('shard')
- norm_grad: float32 [512, 4], P('shard')
- qkv_momentum: float32 [512, 1536], P('shard')
- out_momentum: float32 [512, 512], P('shard')
- up_momentum: float32 [512, 2048], P('shard')
- down_momentum: float32 [2048, 512], P('shard')
- norm_momentum: float32 [512, 4], P('shard')
- qkv_smooth: float32 [512, 1536], P('shard')
- out_smooth: float32 [512, 512], P('shard')
- up_smooth: float32 [512, 2048], P('shard')
- down_smooth: float32 [2048, 512], P('shard')
- norm_smooth: float32 [512, 4], P('shard')
- qkv_updated: float32 [512, 1536], P('shard')
- out_updated: float32 [512, 512], P('shard')
- up_updated: float32 [512, 2048], P('shard')
- down_updated: float32 [2048, 512], P('shard')
- norm_updated: float32 [512, 4], P('shard')
- lifted_grads: float32 [512, 2], P('shard')
Inputs may be any that keep to these rules, and one draw needn't show every extreme that they name: `doc_ids`: each stream's row names the documents of its 512 compressed slots, then its 512 memory slots, then its 768 segment tokens; ids never fall along a row. `norm_params`: columns 0 and 2 hold gains, columns 1 and 3 shifts. `norm_average`: columns 0 and 2 hold gains, columns 1 and 3 shifts.
All inputs are finite; a program needn't handle non-finite values.
Results may differ from a plain program's by a relative error of at most 0.012.
The roundings to bfloat16 on the way count: a program that leaves them out, or rounds other values in their place, can miss the bound.
Values may be sent and summed in bfloat16 or wider, within the bound.
A program may use at most 192 MiB of HBM per device.

v0:
```python
from functools import partial

import jax
import jax.numpy as jnp
from jax import lax
from jax.sharding import PartitionSpec as P

HEADS = 8


MOMENTUM = 0.9
RATE = 0.0025
SMOOTH = 0.8
NEGATIVE = -1e30


def norm_rows(values, gain, shift):
    center = values - jnp.mean(values, axis=-1, keepdims=True)
    spread = jnp.mean(center * center, axis=-1, keepdims=True)
    return center * lax.rsqrt(spread + 1e-05) * gain + shift


def renew(grad_total, moment, average, master):
    momentum = MOMENTUM * moment + (1.0 - MOMENTUM) * grad_total
    updated = master - RATE * ((1.0 - MOMENTUM) * grad_total + MOMENTUM * momentum)
    smooth = SMOOTH * average + (1.0 - SMOOTH) * updated
    return (momentum, smooth, updated)


def split_heads(matrix, head_count):
    return matrix.reshape(matrix.shape[0], head_count, -1).transpose(1, 0, 2)


def merge_heads(stacked_heads):
    return stacked_heads.transpose(1, 0, 2).reshape(stacked_heads.shape[1], -1)


def on_device(
    tokens,
    memory,
    cmemory,
    doc_ids,
    cotangent,
    qkv_weight,
    out_weight,
    up_weight,
    down_weight,
    conv_weight,
    norm_params,
    qkv_moment,
    out_moment,
    up_moment,
    down_moment,
    norm_moment,
    qkv_average,
    out_average,
    up_average,
    down_average,
    norm_average,
):
    wide = jnp.float32
    narrow = jnp.bfloat16
    gathered = (
        lax.all_gather(qkv_weight.astype(narrow), "shard", axis=0, tiled=True),
        lax.all_gather(out_weight.astype(narrow), "shard", axis=0, tiled=True),
        lax.all_gather(up_weight.astype(narrow), "shard", axis=0, tiled=True),
        lax.all_gather(down_weight.astype(narrow), "shard", axis=0, tiled=True),
        lax.all_gather(conv_weight.astype(narrow), "shard", axis=0, tiled=True),
        lax.all_gather(norm_params.astype(narrow), "shard", axis=0, tiled=True),
    )
    qkv_full, out_full, up_full, down_full, conv_full, norm_full = gathered
    segment_in = tokens[0]
    recent = memory[0]
    older = cmemory[0]
    documents = doc_ids[0]
    incoming = cotangent[0]
    segment_len = segment_in.shape[0]
    model_width = segment_in.shape[1]
    history = recent.shape[0] + older.shape[0]
    head_count = HEADS
    head_size = model_width // head_count
    scaling = head_size ** (-0.5)
    stacked = jnp.concatenate([older, recent, segment_in], axis=0).astype(wide)
    length = stacked.shape[0]
    norm_gains = norm_full.astype(wide)
    normed = norm_rows(stacked, norm_gains[:, 0], norm_gains[:, 1]).astype(narrow)
    queries = jnp.dot(
        normed[history:], qkv_full[:, :model_width], preferred_element_type=wide
    ).astype(narrow)
    keyvals = jnp.dot(normed, qkv_full[:, model_width:], preferred_element_type=wide).astype(narrow)
    places = jnp.arange(length)
    allowed = (documents[history:, None] == documents[None, :]) & (
        places[None, :] <= places[history:, None]
    )
    head_queries = split_heads(queries, head_count)
    head_keys = split_heads(keyvals[:, :model_width], head_count)
    head_values = split_heads(keyvals[:, model_width:], head_count)

    def scores_of(query_part, key_part):
        raw_scores = (
            jnp.einsum("qd,kd->qk", query_part, key_part, preferred_element_type=wide) * scaling
        )
        return jnp.where(allowed, raw_scores, NEGATIVE)

    def attend(inputs):
        query_part, key_part, value_part = inputs
        scores = scores_of(query_part, key_part)
        maximum = jnp.max(scores, axis=1, keepdims=True)
        exponent = jnp.exp(scores - maximum)
        summed = jnp.sum(exponent, axis=1, keepdims=True)
        probability = exponent / summed
        attended = jnp.dot(probability.astype(narrow), value_part, preferred_element_type=wide)
        return (attended.astype(narrow), maximum + jnp.log(summed))

    head_attended, log_totals = lax.map(attend, (head_queries, head_keys, head_values))
    attended = merge_heads(head_attended)
    branch = jnp.dot(attended, out_full, preferred_element_type=wide)
    residual = segment_in.astype(wide) + branch
    lifted = norm_rows(residual, norm_gains[:, 2], norm_gains[:, 3]).astype(narrow)
    hidden = jnp.dot(lifted, up_full, preferred_element_type=wide)
    active = jax.nn.gelu(hidden, approximate=True).astype(narrow)
    result = residual + jnp.dot(active, down_full, preferred_element_type=wide)
    output = result.astype(narrow)
    evicted = jnp.concatenate([recent, segment_in], axis=0)[:segment_len].reshape(
        segment_len // 3, 3 * model_width
    )
    squeezed = jnp.dot(evicted, conv_full, preferred_element_type=wide).astype(narrow)
    new_older = jnp.concatenate([older[segment_len // 3 :], squeezed], axis=0)
    new_recent = segment_in[segment_len - recent.shape[0] :]
    again = (
        lax.all_gather(qkv_weight.astype(narrow), "shard", axis=0, tiled=True),
        lax.all_gather(out_weight.astype(narrow), "shard", axis=0, tiled=True),
        lax.all_gather(up_weight.astype(narrow), "shard", axis=0, tiled=True),
        lax.all_gather(down_weight.astype(narrow), "shard", axis=0, tiled=True),
        lax.all_gather(norm_params.astype(narrow), "shard", axis=0, tiled=True),
    )
    qkv_back, out_back, up_back, down_back, norm_back = again
    back_gains = norm_back.astype(wide)
    grad_down = jnp.einsum("sf,sd->fd", active, incoming, preferred_element_type=wide)
    grad_active = jnp.einsum("sd,fd->sf", incoming, down_back, preferred_element_type=wide)
    gelu_back = jax.vjp(partial(jax.nn.gelu, approximate=True), hidden)[1]
    grad_hidden = gelu_back(grad_active)[0].astype(narrow)
    grad_up = jnp.einsum("sd,sf->df", lifted, grad_hidden, preferred_element_type=wide)
    grad_lifted = jnp.einsum("sf,df->sd", grad_hidden, up_back, preferred_element_type=wide)
    second_back = jax.vjp(norm_rows, residual, back_gains[:, 2], back_gains[:, 3])[1]
    grad_through, grad_gain_two, grad_shift_two = second_back(grad_lifted)
    grad_residual = incoming.astype(wide) + grad_through
    grad_branch = grad_residual.astype(narrow)
    grad_out = jnp.einsum("sa,sd->ad", attended, grad_branch, preferred_element_type=wide)
    grad_attended = jnp.einsum(
        "sd,ad->sa", grad_branch, out_back, preferred_element_type=wide
    ).astype(narrow)
    head_grads = split_heads(grad_attended, head_count)

    def attend_back(inputs):
        query_part, key_part, value_part, grad_part, log_total = inputs
        scores = scores_of(query_part, key_part)
        probability = jnp.exp(scores - log_total)
        grad_prob = jnp.einsum("qd,kd->qk", grad_part, value_part, preferred_element_type=wide)
        weighted = jnp.sum(probability * grad_prob, axis=1, keepdims=True)
        grad_scores = (probability * (grad_prob - weighted)).astype(narrow)
        grad_query = jnp.dot(grad_scores, key_part, preferred_element_type=wide) * scaling
        grad_key = (
            jnp.einsum("qk,qd->kd", grad_scores, query_part, preferred_element_type=wide) * scaling
        )
        grad_value = jnp.einsum(
            "qk,qd->kd", probability.astype(narrow), grad_part, preferred_element_type=wide
        )
        return (grad_query.astype(narrow), grad_key.astype(narrow), grad_value.astype(narrow))

    head_gq, head_gk, head_gv = lax.map(
        attend_back, (head_queries, head_keys, head_values, head_grads, log_totals)
    )
    grad_queries = merge_heads(head_gq)
    grad_keyvals = jnp.concatenate([merge_heads(head_gk), merge_heads(head_gv)], axis=1)
    grad_qkv = jnp.concatenate(
        [
            jnp.einsum("sd,se->de", normed[history:], grad_queries, preferred_element_type=wide),
            jnp.einsum("ld,le->de", normed, grad_keyvals, preferred_element_type=wide),
        ],
        axis=1,
    )
    grad_normed = jnp.einsum(
        "le,de->ld", grad_keyvals, qkv_back[:, model_width:], preferred_element_type=wide
    )
    query_part_grad = jnp.einsum(
        "se,de->sd", grad_queries, qkv_back[:, :model_width], preferred_element_type=wide
    )
    grad_normed = grad_normed + jnp.concatenate(
        [jnp.zeros((history, model_width), wide), query_part_grad], axis=0
    )
    first_back = jax.vjp(norm_rows, stacked, back_gains[:, 0], back_gains[:, 1])[1]
    grad_rows, grad_gain_one, grad_shift_one = first_back(grad_normed)
    token_grad = (grad_residual + grad_rows[history:]).astype(narrow)
    grad_norm = jnp.stack([grad_gain_one, grad_shift_one, grad_gain_two, grad_shift_two], axis=1)
    shares = (
        lax.psum_scatter(grad_qkv, "shard", scatter_dimension=0, tiled=True),
        lax.psum_scatter(grad_out, "shard", scatter_dimension=0, tiled=True),
        lax.psum_scatter(grad_up, "shard", scatter_dimension=0, tiled=True),
        lax.psum_scatter(grad_down, "shard", scatter_dimension=0, tiled=True),
        lax.psum_scatter(grad_norm, "shard", scatter_dimension=0, tiled=True),
    )
    qkv_total, out_total, up_total, down_total, norm_total = lax.psum(
        (shares[0], shares[1], shares[2], shares[3], shares[4]), "stream"
    )
    qkv_new = renew(qkv_total, qkv_moment, qkv_average, qkv_weight)
    out_new = renew(out_total, out_moment, out_average, out_weight)
    up_new = renew(up_total, up_moment, up_average, up_weight)
    down_new = renew(down_total, down_moment, down_average, down_weight)
    norm_new = renew(norm_total, norm_moment, norm_average, norm_params)
    lifted_grads = norm_total[:, 2:4]
    return (
        output[None],
        new_recent[None],
        new_older[None],
        token_grad[None],
        qkv_total,
        out_total,
        up_total,
        down_total,
        norm_total,
        qkv_new[0],
        out_new[0],
        up_new[0],
        down_new[0],
        norm_new[0],
        qkv_new[1],
        out_new[1],
        up_new[1],
        down_new[1],
        norm_new[1],
        qkv_new[2],
        out_new[2],
        up_new[2],
        down_new[2],
        norm_new[2],
        lifted_grads,
    )


def solution(mesh):
    return jax.shard_map(
        on_device,
        mesh=mesh,
        in_specs=(
            P(("stream", "shard"), None, None),
            P(("stream", "shard"), None, None),
            P(("stream", "shard"), None, None),
            P(("stream", "shard"), None),
            P(("stream", "shard"), None, None),
            P("shard", None),
            P("shard", None),
            P("shard", None),
            P("shard", None),
            P("shard", None),
            P("shard", None),
            P("shard", None),
            P("shard", None),
            P("shard", None),
            P("shard", None),
            P("shard", None),
            P("shard", None),
            P("shard", None),
            P("shard", None),
            P("shard", None),
            P("shard", None),
        ),
        out_specs=(
            P(("stream", "shard"), None, None),
            P(("stream", "shard"), None, None),
            P(("stream", "shard"), None, None),
            P(("stream", "shard"), None, None),
            P("shard", None),
            P("shard", None),
            P("shard", None),
            P("shard", None),
            P("shard", None),
            P("shard", None),
            P("shard", None),
            P("shard", None),
            P("shard", None),
            P("shard", None),
            P("shard", None),
            P("shard", None),
            P("shard", None),
            P("shard", None),
            P("shard", None),
            P("shard", None),
            P("shard", None),
            P("shard", None),
            P("shard", None),
            P("shard", None),
            P("shard", None),
        ),
        check_vma=False,
    )
```

profile of v0, /device:TPU:0, one launch (start us, length us, event | category | flops | bytes accessed | tf_op | source)
XLA Modules:
  0.0 630.7 jit_solution(3189794009569891588)
XLA Ops:
  7.3 2.5 convert_element_type.95
  11.1 2.7 convert_element_type.102
  14.0 5.4 all_gather.23
  19.5 14.2 %all_gather.25 = bf16[512,512]{1,0:T(8,128)(2,1)} all-gather(bf16[256,512]{1,0:T(8,128)(2,1)S(1)} %convert_element_type.98), channel_id=1, replica_groups=mesh['stream'=16,'shard'=2] {'shard'}, dimensions={0}, use_global_device_ids=true | all-gather | bytes 786432 | tf_op jit(solution)/shard_map/all_gather | solution.py:65
  38.2 6.3 all-gather.5.cloned.1.call-done
  44.5 2.8 convolution_convert_fusion.2
  47.2 2.6 copy.82
  49.8 3.3 convolution_convert_fusion
  54.6 4.7 copy.83
  59.3 3.0 copy.84
  62.3 47.6 %while.28 = (s32[]{:T(128)}, bf16[8,768,64]{1,2,0:T(8,128)(2,1)S(1)}, f32[8,768,1]{1,2,0:T(1,128)S(1)}, bf16[8,768,64]{2,1,0:T(8,128)(2,1)}, bf16[8,1792,64]{2,1...) while((s32[]{:T(128)}, ...), condition=%wide.region_5.6_spmd.clone, body=%wide.region_2.5_spmd.clone.sunk | while | flops 367508736 | bytes 17776752 | solution.py:115
  62.3 2.7 fusion.142
  65.9 2.3 fusion.144
  68.3 2.7 fusion.142
  71.9 2.3 fusion.144
  74.2 2.7 fusion.142
  77.8 2.3 fusion.144
  80.2 2.7 fusion.142
  83.8 2.3 fusion.144
  86.1 2.7 fusion.142
  89.7 2.3 fusion.144
  92.1 2.8 fusion.142
  95.8 2.3 fusion.144
  98.1 2.7 fusion.142
  101.7 2.3 fusion.144
  104.0 2.7 fusion.142
  107.6 2.3 fusion.144
  113.0 6.2 fusion.96
  119.2 7.9 %fusion.62 = bf16[768,2048]{1,0:T(8,128)(2,1)S(1)} fusion(f32[768,2048]{1,0:T(8,128)} %fusion.96, bf16[2048,512]{1,0:T(8,128)(2,1)} %all-gather.9.cloned.1.call-done, bf16[1,768,512]{2,1,0:T(8,128)(2,1)} %param.29), kind=kOutput, calls=%fused_computation.69 | convolution fusion | flops 1642070016 | bytes 12320768 | tf_op jit(solution)/shard_map/sd,fd->sf/dot_general | solution.py:140
  127.2 3.0 fusion.103
  130.2 3.0 copy.88
  139.5 2.6 convolution_convert_fusion.1
  142.2 2.4 copy.89
  144.7 101.4 %while.29 = (s32[]{:T(128)}, bf16[8,768,64]{1,2,0:T(8,128)(2,1)S(1)}, bf16[8,1792,64]{1,2,0:T(8,128)(2,1)}, bf16[8,1792,64]{1,2,0:T(8,128)(2,1)}, bf16[8,768,64]...) while((s32[]{:T(128)}, ...), condition=%wide.region_12.13_spmd.clone, body=%wide.region_10.12_spmd.clone.sunk | while | flops 897760512 | bytes 44041352 | solution.py:171
  146.8 3.5 multiply_reduce_fusion.5
  155.1 2.3 fusion.155
  159.4 3.5 multiply_reduce_fusion.5
  163.5 2.3 fusion.156
  172.1 3.5 multiply_reduce_fusion.5
  184.8 3.5 multiply_reduce_fusion.5
  197.5 3.5 multiply_reduce_fusion.5
  210.1 3.5 multiply_reduce_fusion.5
  222.8 3.5 multiply_reduce_fusion.5
  235.5 3.5 multiply_reduce_fusion.5
  248.2 4.1 fusion.74
  255.5 7.8 %fusion.82 = f32[2048,512]{1,0:T(8,128)} fusion(bf16[1,768,512]{2,1,0:T(8,128)(2,1)S(1)} %copy-done.34, f32[768,2048]{1,0:T(8,128)} %fusion.96), kind=kOutput, calls=%fused_computation.120 | convolution fusion | flops 1624768512 | bytes 11272192 | tf_op jit(solution)/shard_map/sf,sd->fd/dot_general | solution.py:139
  263.3 5.8 fusion.95
  269.3 2.4 convert_element_type.104
  273.9 6.4 %fusion.71 = (f32[512]{0:T(512)S(1)}, f32[1792]{0:T(1024)S(1)}, f32[512]{0:T(512)S(1)}, f32[1792,512]{0,1:T(8,128)}) fusion(f32[1792]{0:T(1024)S(1)} %copy-done.42, f32[1792]{0:T(1024)S(1)} %copy-done.40, bf16[768,512]{0,1:T(8,128)(2,1)S(1)} %bitcast.156, bf16[512,512]{0,1:T(8,128)(2,1)S(1)} %bitcast.162, bf16[512,512]{0,1:T(8,128)(2,1)S(1)} %bitcast.168, ...), kind=kOutput, calls=%fused_computation.83 | convolution fusion | flops 1900147968 | bytes 11826176 | tf_op jit(solution)/shard_map/le,de->ld/dot_general | solution.py:183
  283.3 15.8 %reduce-scatter.8.cloned.1.call-done = f32[256,1536]{1,0:T(8,128)} async-done(((f32[512,1536]{1,0:T(8,128)}), f32[256,1536]{1,0:T(8,128)}) %reduce-scatter.8.cloned.1.call-update) | async-done | bytes 1572880 | tf_op jit(solution)/shard_map/reduce_scatter | solution.py:197
  299.1 56.5 %reduce-scatter.14.cloned.1.call-done = f32[1024,512]{1,0:T(8,128)} async-done(((f32[2048,512]{1,0:T(8,128)}), f32[1024,512]{1,0:T(8,128)}) %reduce-scatter.14.cloned.1.call-update) | async-done | bytes 2097168 | tf_op jit(solution)/shard_map/reduce_scatter | solution.py:200
  355.6 56.7 %reduce-scatter.12.cloned.1.call-done = f32[256,2048]{1,0:T(8,128)} async-done(((f32[512,2048]{1,0:T(8,128)}), f32[256,2048]{1,0:T(8,128)}) %reduce-scatter.12.cloned.1.call-update) | async-done | bytes 2097168 | tf_op jit(solution)/shard_map/reduce_scatter | solution.py:199
  413.3 2.3 copy.86
  419.4 22.3 %all-gather.11.cloned.1.call-done = bf16[1536,512]{1,0:T(8,128)(2,1)} async-done(((bf16[768,512]{1,0:T(8,128)(2,1)}), bf16[1536,512]{1,0:T(8,128)(2,1)}) %all-gather.11.cloned.1.call-update) | async-done | bytes 1572880 | tf_op jit(solution)/shard_map/all_gather | solution.py:68
  441.7 2.4 convolution_convert_fusion.3
  444.9 6.4 %fusion.77 = bf16[1,768,512]{1,2,0:T(8,128)(2,1)} fusion(f32[768,512]{0,1:T(8,128)S(1)} %get-tuple-element.330, bf16[2048,512]{1,0:T(8,128)(2,1)S(1)} %copy-done.53, f32[768,2048]{1,0:T(8,128)} %fusion.96), kind=kOutput, calls=%fused_computation.113 | convolution fusion | flops 1625554944 | bytes 10747904 | tf_op jit(solution)/shard_map/dot_general | solution.py:122
  451.4 2.3 copy.94
  453.7 2.9 fusion.97
  459.4 34.8 %psum.39 = f32[256,4]{0,1:T(4,128)S(1)} all-reduce(f32[256,4]{0,1:T(4,128)S(1)} %copy.101), channel_id=1, replica_groups=mesh['stream'=16,'shard'=2] {'stream'}, use_global_device_ids=true, to_apply=%region_28.29 | all-reduce | flops 1024 | bytes 8192 | tf_op jit(solution)/shard_map/psum | solution.py:203
  495.4 105.6 %all-reduce.4.cloned.1.call-done = (f32[256,1536]{1,0:T(8,128)}, f32[256,512]{1,0:T(8,128)}, f32[256,2048]{1,0:T(8,128)}, f32[1024,512]{1,0:T(8,128)}) async-done(((f32[256,1536]{1,0:T(8,128)}, f32[256,512]{1,0:T(8,128)}, f32[256,2048]{1,0:T(8,128)}, f32[1024,512]{1,0:T(8,128)}), (f32[256,1536]{1,0:T(8,128)}, f32[256,512]{1,0:T(8,128)}, f32[256,2048]{1,0:T(8,128)}, ...) | async-done | bytes 6291472 | tf_op jit(solution)/shard_map/psum | solution.py:203
  601.0 2.5 multiply_add_fusion.6
  603.5 5.1 multiply_add_fusion.4
  609.6 4.4 multiply_add_fusion.1
  615.3 3.6 multiply_add_fusion
  (260 shorter events, 119.4 us)
Async XLA Ops:
  7.2 2.6 copy-start.7
  7.2 37.2 %all-gather.5.cloned.1.call-start = ((), (), s32[]{:S(2)}) async-start(), calls=%async_computation.5 | async-start | bytes 2359296 | tf_op jit(solution)/shard_map/all_gather | solution.py:64
  9.8 103.2 %all-gather.7.cloned.1.call-start = ((), (), s32[]{:S(2)}) async-start(), calls=%async_computation.6 | async-start | bytes 3145728 | tf_op jit(solution)/shard_map/all_gather | solution.py:66
  11.0 2.9 copy-start.50
  11.0 3.0 copy-start.48
  11.0 8.4 %copy-start.27 = (f32[256,512]{1,0:T(8,128)S(1)}, f32[256,512]{1,0:T(8,128)}, u32[]{:S(2)}) copy-start(f32[256,512]{1,0:T(8,128)} %param.31) | copy-start | bytes 1572868
  11.0 108.2 %all-gather.9.cloned.1.call-start = ((), (), s32[]{:S(2)}) async-start(), calls=%async_computation.7 | async-start | bytes 3145728 | tf_op jit(solution)/shard_map/all_gather | solution.py:67
  13.8 19.9 %copy-start.37 = (bf16[1,512,512]{2,1,0:T(8,128)(2,1)S(1)}, bf16[1,512,512]{2,1,0:T(8,128)(2,1)}, u32[]{:S(2)}) copy-start(bf16[1,512,512]{2,1,0:T(8,128)(2,1)} %param.26) | copy-start | bytes 1572868
  13.8 20.1 %copy-start.31 = (bf16[1,512,512]{2,1,0:T(8,128)(2,1)S(1)}, bf16[1,512,512]{2,1,0:T(8,128)(2,1)}, u32[]{:S(2)}) copy-start(bf16[1,512,512]{2,1,0:T(8,128)(2,1)} %param.27) | copy-start | bytes 1572868
  13.9 20.3 %copy-start.22 = (bf16[1,768,512]{2,1,0:T(8,128)(2,1)S(1)}, bf16[1,768,512]{2,1,0:T(8,128)(2,1)}, u32[]{:S(2)}) copy-start(bf16[1,768,512]{2,1,0:T(8,128)(2,1)} %param.25) | copy-start | bytes 2359300
  13.9 269.4 %reduce-scatter.10.cloned.1.call-start = ((), (), s32[]{:S(2)}) async-start(), calls=%async_computation.10 | async-start | bytes 1572864 | tf_op jit(solution)/shard_map/reduce_scatter | solution.py:198
  19.4 16.8 %copy-start.46 = (f32[512,1]{0,1:T(1,128)}, f32[512,1]{0,1:T(1,128)S(1)}, u32[]{:S(2)}) copy-start(f32[512,1]{0,1:T(1,128)S(1)} %get-tuple-element.327) | copy-start | bytes 6148
  33.9 2.3 copy-start
  34.2 2.1 copy-start.5
  34.4 1.4 copy-start.33
  34.8 3.4 copy-start.39
  35.9 2.3 copy-start.41
  36.2 99.5 %copy-start.12 = (bf16[1,768,512]{1,2,0:T(8,128)(2,1)}, bf16[1,768,512]{1,2,0:T(8,128)(2,1)S(1)}, u32[]{:S(2)}) copy-start(bf16[1,768,512]{1,2,0:T(8,128)(2,1)S(1)} %copy.87) | copy-start | bytes 2359300
  38.2 11.7 %copy-start.19 = (bf16[1792,512]{0,1:T(8,128)(2,1)S(1)}, bf16[1792,512]{0,1:T(8,128)(2,1)}, u32[]{:S(2)}) copy-start(bf16[1792,512]{0,1:T(8,128)(2,1)} %fusion.70) | copy-start | bytes 5505028
  110.0 0.9 copy-start.15
  119.2 7.9 %copy-start.54 = (bf16[512,2048]{1,0:T(8,128)(2,1)S(1)}, bf16[512,2048]{1,0:T(8,128)(2,1)}, u32[]{:S(2)}) copy-start(bf16[512,2048]{1,0:T(8,128)(2,1)} %all-gather.7.cloned.1.call-done) | copy-start | bytes 6291460
  127.2 3.0 copy-start.55
  133.2 2.0 copy-start.2
  135.7 1.1 copy-start.3
  135.7 2.3 copy-start.16
  138.0 1.6 copy-start.30
  142.1 157.0 %reduce-scatter.8.cloned.1.call-start = ((), (), s32[]{:S(2)}) async-start(), calls=%async_computation.9 | async-start | bytes 4718592 | tf_op jit(solution)/shard_map/reduce_scatter | solution.py:197
  246.1 6.2 copy-start.14
  246.1 2.1 copy-start.20
  254.3 1.1 copy-start.34
  254.3 101.2 %reduce-scatter.14.cloned.1.call-start = ((), (), s32[]{:S(2)}) async-start(), calls=%async_computation.12 | async-start | bytes 6291456 | tf_op jit(solution)/shard_map/reduce_scatter | solution.py:200
  263.3 149.0 %reduce-scatter.12.cloned.1.call-start = ((), (), s32[]{:S(2)}) async-start(), calls=%async_computation.11 | async-start | bytes 6291456 | tf_op jit(solution)/shard_map/reduce_scatter | solution.py:199
  269.2 172.5 %all-gather.11.cloned.1.call-start = ((), (), s32[]{:S(2)}) async-start(), calls=%async_computation.8 | async-start | bytes 2359296 | tf_op jit(solution)/shard_map/all_gather | solution.py:68
  271.7 2.1 copy-start.1
  271.7 2.1 copy-start.6
  271.7 2.1 copy-start.40
  271.7 2.2 copy-start.42
  271.7 2.2 copy-start.47
  271.7 186.6 %reduce-scatter.16.cloned.1.call-start = ((), (), s32[]{:S(2)}) async-start(), calls=%async_computation.13 | async-start | bytes 393216
  271.8 2.1 copy-start.38
  281.2 319.8 %all-reduce.4.cloned.1.call-start = ((), (), s32[]{:S(2)}) async-start(), calls=%async_computation.14 | async-start | bytes 12582912 | tf_op jit(solution)/shard_map/psum | solution.py:203
  441.7 2.4 copy-start.32
  441.7 3.2 copy-start.53
  444.9 8.7 %copy-start.44 = (f32[1792]{0:T(1024)S(1)}, f32[1792]{0:T(1024)}, u32[]{:S(2)}) copy-start(f32[1792]{0:T(1024)} %copy-done.43) | copy-start | bytes 21508
  453.7 2.9 copy-start.4
  453.7 2.9 copy-start.13
  456.6 38.1 %copy-start.49 = (f32[256,4]{0,1:T(4,128)S(1)}, f32[256,4]{0,1:T(4,128)}, u32[]{:S(2)}) copy-start(f32[256,4]{0,1:T(4,128)} %param.35) | copy-start | bytes 12292
  456.6 38.1 %copy-start.51 = (f32[256,4]{0,1:T(4,128)S(1)}, f32[256,4]{0,1:T(4,128)}, u32[]{:S(2)}) copy-start(f32[256,4]{0,1:T(4,128)} %param.45) | copy-start | bytes 12292
  456.6 38.1 %copy-start.52 = (f32[256,4]{0,1:T(4,128)S(1)}, f32[256,4]{0,1:T(4,128)}, u32[]{:S(2)}) copy-start(f32[256,4]{0,1:T(4,128)} %param.40) | copy-start | bytes 12292
  456.7 144.3 %copy-start.28 = (f32[256,512]{1,0:T(8,128)S(1)}, f32[256,512]{1,0:T(8,128)}, u32[]{:S(2)}) copy-start(f32[256,512]{1,0:T(8,128)} %param.31) | copy-start | bytes 1572868
  456.7 144.3 %copy-start.35 = (f32[256,512]{1,0:T(8,128)S(1)}, f32[256,512]{1,0:T(8,128)}, u32[]{:S(2)}) copy-start(f32[256,512]{1,0:T(8,128)} %param.42) | copy-start | bytes 1572868
  457.1 143.9 %copy-start.36 = (f32[256,512]{1,0:T(8,128)S(1)}, f32[256,512]{1,0:T(8,128)}, u32[]{:S(2)}) copy-start(f32[256,512]{1,0:T(8,128)} %param.37) | copy-start | bytes 1572868
  458.3 145.2 %copy-start.17 = (f32[256,1536]{1,0:T(8,128)S(1)}, f32[256,1536]{1,0:T(8,128)}, u32[]{:S(2)}) copy-start(f32[256,1536]{1,0:T(8,128)} %param.30) | copy-start | bytes 4718596
  494.2 114.4 %copy-start.45 = (f32[256,4]{0,1:T(4,128)}, f32[256,4]{0,1:T(4,128)S(1)}, u32[]{:S(2)}) copy-start(f32[256,4]{0,1:T(4,128)S(1)} %psum.39) | copy-start | bytes 12292
  601.0 2.5 copy-start.18
  603.5 5.1 copy-start.8
  603.5 5.1 copy-start.11
  603.5 5.1 copy-start.23
  603.5 6.1 copy-start.24
  609.6 4.4 copy-start.9
  609.6 4.4 copy-start.10
  609.6 4.4 copy-start.25
  609.6 5.7 copy-start.26
  618.9 1.4 copy-start.29
  (2 other events, 1.5 us)
Sparse Core Ops, SparseCore 0:
  10.2 34.2 all-gather.4
  46.6 34.3 all-gather.6
  83.1 33.0 all-gather.8
  142.3 21.5 reduce-scatter.9
  254.5 44.5 reduce-scatter.7
  301.3 54.2 reduce-scatter.13
  358.0 54.3 reduce-scatter.11
  414.4 27.2 all-gather.10
  444.5 11.6 reduce-scatter.15
  460.5 140.3 all-reduce.3
where the time goes:
time: 637 us; the launch traced here: 631 us
  waiting for transfers between devices  263 us (41%)
  matrix products  203 us (32%)
  blocking collectives  54.4 us (9%)
  other arithmetic  49 us (8%)
  local copies, waits for them, and re-layouts  44 us (7%)
  between operations  15.1 us (2%)
    psum x1, waiting for transfers between devices, on_device(): lax.psum((shares[0], shares[1], shares[2], shares[3], shares[4]), 'stream')  106 us
    reduce_scatter x1, waiting for transfers between devices, on_device(): lax.psum_scatter(grad_up, 'shard', scatter_dimension=0, tiled=True)  56.7 us
    reduce_scatter x1, waiting for transfers between devices, on_device(): lax.psum_scatter(grad_down, 'shard', scatter_dimension=0, tiled=True)  56.5 us
    dot_general x16, matrix products, scores_of(): jnp.einsum('qd,kd->qk', query_part, key_part, preferred_element_type=wide)  50 us
    psum x1, blocking collectives, on_device(): lax.psum((shares[0], shares[1], shares[2], shares[3], shares[4]), 'stream')  34.8 us
    all_gather x1, waiting for transfers between devices, on_device(): lax.all_gather(conv_weight.astype(narrow), 'shard', axis=0, tiled=True)  22.3 us
    dot_general x8, matrix products, attend(): jnp.dot(probability.astype(narrow), value_part, preferred_element_type=wide)  18.4 us
    dot_general x8, matrix products, attend_back(): jnp.einsum('qk,qd->kd', probability.astype(narrow), grad_part, preferred_...  18.3 us
  transfers between devices with their start and end apart: 10, of which 6 were waited for; matrix products, arithmetic and copies ran while one was open for 39% of the time, Pallas kernels for 0%

commit v1 on v0

v1 whole, which is shorter than its diff:
```python
import functools

import jax
import jax.numpy as jnp
from jax import lax
from jax.experimental import pallas as pl
from jax.experimental.pallas import tpu as pltpu
from jax.sharding import PartitionSpec as P

HEADS = 8
MOMENTUM = 0.9
RATE = 0.0025
SMOOTH = 0.8
REACH = 448
BF = jnp.bfloat16
F32 = jnp.float32
MESH = pl.DeviceIdType.MESH
GELU_C = 0.7978845608028654
GELU_A = 0.044715


def nn(a, b):
    return lax.dot_general(a, b, (((1,), (0,)), ((), ())), preferred_element_type=F32)


def nt(a, b):
    return lax.dot_general(a, b, (((1,), (1,)), ((), ())), preferred_element_type=F32)


def tn(a, b):
    return lax.dot_general(a, b, (((0,), (0,)), ((), ())), preferred_element_type=F32)


def normalised(x):
    center = x - jnp.mean(x, axis=-1, keepdims=True)
    scale = lax.rsqrt(jnp.mean(center * center, axis=-1, keepdims=True) + 1e-5)
    return center * scale, scale


def norm_back(grad, unit, scale, gain):
    inner = grad * gain
    first = jnp.mean(inner, axis=-1, keepdims=True)
    second = jnp.mean(inner * unit, axis=-1, keepdims=True)
    return (inner - first - unit * second) * scale


def two_heads(block):
    lane = lax.broadcasted_iota(jnp.int32, block.shape, 1)
    zero = jnp.zeros_like(block)
    low = lane < 64
    return jnp.concatenate([jnp.where(low, block, zero), jnp.where(low, zero, block)], axis=0)


def own_halves(block):
    return jnp.concatenate([block[0:64, 0:128], block[64:128, 128:256]], axis=0)


def rows_at(start, count, by=16):
    return pl.ds(pl.multiple_of(start, by), count)


class Sems:
    def __init__(self, ref, size):
        self.ref, self.size, self.used = ref, size, 0

    def take(self):
        self.used += 1
        assert self.used <= self.size
        return self.ref.at[self.used - 1]


class Place:
    def __init__(self, streams, shards):
        self.streams, self.shards = streams, shards
        self.s = lax.axis_index("stream")
        self.y = lax.axis_index("shard")
        self.bits = []
        bit = 1
        while bit < streams:
            self.bits.append(bit)
            bit *= 2

    def bit(self, bit):
        return (self.s // bit) % 2

    def across(self, bit):
        return (self.s + bit * (1 - 2 * self.bit(bit)), self.y)

    def shard_bit(self, bit):
        return (self.y // bit) % 2

    def shard_across(self, bit):
        return (self.s, self.y + bit * (1 - 2 * self.shard_bit(bit)))

    def ahead(self, j):
        return (self.s, (self.y + j) % self.shards)

    def behind(self, j):
        return (self.y + self.shards - j) % self.shards


def remote(src, dst, sems, who):
    copy = pltpu.make_async_remote_copy(
        src_ref=src, dst_ref=dst, send_sem=sems[0], recv_sem=sems[1], device_id=who, device_id_type=MESH
    )
    copy.start()
    return copy


class Gather:
    def __init__(self, place, buf, send, recv, split):
        self.p, self.buf, self.send, self.recv = place, buf, send, recv
        self.rows = buf.shape[0] // place.shards
        self.split = split
        self.count = self.rows // (4 if split else 2)
        core, near = place.bit(1), place.bit(2)
        self.core, self.near = core, near
        self.part = near * 2 + core if split else core
        self.first, self.second, self.third = [], [], []

    def view(self, owner, part):
        return self.buf.at[rows_at(owner * self.rows + part * self.count, self.count), :]

    def sems(self):
        return self.send.take(), self.recv.take()

    def start(self):
        for j in range(1, self.p.shards):
            v = self.view(self.p.y, self.part)
            self.first.append(remote(v, v, self.sems(), self.p.ahead(j)))

    def spread(self):
        for j in range(1, self.p.shards):
            self.first[j - 1].wait_recv()
            v = self.view(self.p.behind(j), self.part)
            if self.split:
                self.second.append(remote(v, v, self.sems(), self.p.across(2)))
            self.third.append(remote(v, v, self.sems(), self.p.across(1)))

    def pass_on(self):
        if self.split:
            for j in range(1, self.p.shards):
                self.second[j - 1].wait_recv()
                v = self.view(self.p.behind(j), (1 - self.near) * 2 + self.core)
                self.third.append(remote(v, v, self.sems(), self.p.across(1)))

    def finish(self):
        for copy in self.third:
            copy.wait_recv()

    def sent(self):
        for copy in self.first + self.second + self.third:
            copy.wait_send()


class Total:
    def __init__(self, place, grad, total, slots, send, recv, order):
        self.p, self.grad, self.total = place, grad, total
        self.send, self.recv = send, recv
        self.slots = list(slots)
        self.order = [("stream", 1)] + list(order)
        rows = grad.shape[0] // place.shards
        self.rows = rows
        self.blocks = [(j * rows, j) for j in range(place.shards)]
        self.count = rows
        self.back = []
        self.live = []
        self.done = []
        self.stage = -1
        self.held = []

    def sems(self):
        return self.send.take(), self.recv.take()

    def n_steps(self):
        return 0

    def begin(self):
        axis, bit = self.order[self.stage]
        slot = self.slots.pop(0)
        self.live, self.held = [], []
        if axis == "stream":
            mine = self.p.bit(bit)
            halve = self.count % 32 == 0
            keep = self.count // 2 if halve else self.count
            for n, start in enumerate(self.starts):
                gone = start + (1 - mine) * keep if halve else start
                kept = start + mine * keep if halve else start
                src = self.grad.at[rows_at(gone, keep), :]
                dst = slot.at[pl.ds(n * keep, keep), :]
                self.live.append(remote(src, dst, self.sems(), self.p.across(bit)))
                self.held.append(kept)
            if halve:
                self.back.append(bit)
            self.count = keep
        else:
            mine = self.p.shard_bit(bit)
            half = len(self.starts) // 2
            low, high = self.starts[:half], self.starts[half:]
            for n in range(half):
                gone = jnp.where(mine == 0, high[n], low[n])
                kept = jnp.where(mine == 0, low[n], high[n])
                src = self.grad.at[rows_at(gone, self.count), :]
                dst = slot.at[pl.ds(n * self.count, self.count), :]
                self.live.append(remote(src, dst, self.sems(), self.p.shard_across(bit)))
                self.held.append(kept)
        self.slot = slot

    def add(self, last):
        for n, copy in enumerate(self.live):
            copy.wait_recv()
            here = rows_at(self.held[n], self.count)
            value = self.grad[here, :].astype(F32) + self.slot[pl.ds(n * self.count, self.count), :].astype(F32)
            if last:
                self.total[rows_at(self.held[n] - self.p.y * self.rows, self.count), :] = value.astype(BF)
            else:
                self.grad[here, :] = value.astype(BF)
        self.done += self.live
        self.starts = self.held

    def share(self):
        bit = self.back.pop()
        v = self.total.at[rows_at(self.own, self.count), :]
        copy = remote(v, v, self.sems(), self.p.across(bit))
        self.own = self.own - self.p.bit(bit) * self.count
        self.count *= 2
        self.live = [copy]

    def steps(self):
        def first():
            self.starts = [b[0] for b in self.blocks]
            self.stage = 0
            self.begin()

        def middle():
            self.add(False)
            self.stage += 1
            self.begin()

        def turn():
            self.add(True)
            self.own = self.held[0] - self.p.y * self.rows
            self.share()

        def later():
            self.live[0].wait_recv()
            self.done += self.live
            self.share()

        def end():
            self.live[0].wait_recv()
            self.done += self.live

        halvings = len(self.order)
        out = [first] + [middle] * (halvings - 1) + [turn]
        count, shares = self.rows, 0
        for axis, bit in self.order:
            if axis == "stream" and count % 32 == 0:
                count //= 2
                shares += 1
        return out + [later] * (shares - 1) + [end]

    def sent(self):
        for copy in self.done:
            copy.wait_send()


def slot_shapes(place_sizes, rows, columns, order):
    streams, shards = place_sizes
    blocks, count, shapes = shards, rows // shards, []
    for axis, bit in [("stream", 1)] + list(order):
        if axis == "stream":
            if count % 32 == 0:
                count //= 2
        else:
            blocks //= 2
        shapes.append((blocks * count, columns))
    return shapes


def orders(streams, shards):
    upper, lower = [], []
    bit = 2
    while bit < streams:
        upper.append(("stream", bit))
        bit *= 2
    bit = shards // 2
    while bit >= 1:
        lower.append(("shard", bit))
        bit //= 2
    return lower + upper, upper[:1] + lower + upper[1:]


GRADS = ("d0", "d1", "u0", "u1", "o", "qa", "qb")
FFN = ("d0", "u0", "d1", "u1")
LATE = ("qb", "qa", "o") + FFN


def layer_kernel(
    sizes, plan, tok, mem, old, docs, cot, wqkv, wo, wu, wd, wc, norms, out, tgrad, newold, norm_total, *rest
):
    totals = rest[:7]
    (
        xs, N, Q, K, V, PT, OT, bias, res, gres, lifted, act, gh, gl, gr, dO, Dv, dK, dV, ct,
        Wq, Wk, Wv, Wo, Wu, Wd, Wc, nblocks, ngrad, nslots, ev,
    ) = rest[7:38]
    rest = rest[38:]
    gbuf, tbuf = rest[:7], rest[7:14]
    rest = rest[14:]
    slots = []
    for n in plan["slot_counts"]:
        slots.append(rest[:n])
        rest = rest[n:]
    send_ref, recv_ref, local_ref = rest
    place = Place(*sizes)
    send, recv, local = Sems(send_ref, plan["sems"]), Sems(recv_ref, plan["sems"]), Sems(local_ref, plan["local"])
    shards = place.shards
    S, D = tok.shape
    M = mem.shape[0]
    H0 = M - REACH
    L = REACH + S
    T0 = REACH
    W = REACH + 128
    FF = Wu.shape[1]
    n_q = S // 128

    barrier = pltpu.get_barrier_semaphore()
    partners = [place.across(bit) for bit in place.bits] + [place.ahead(j) for j in range(1, shards)]
    for who in partners:
        pl.semaphore_signal(barrier, inc=1, device_id=who, device_id_type=MESH)

    def fetch(src, dst):
        copy = pltpu.make_async_copy(src, dst, local.take())
        copy.start()
        return copy

    pools = [dK, dV, gl, gres, res]
    free = [[ref, 0] for ref in pools]

    def room(rows):
        for entry in free:
            if entry[1] + rows <= entry[0].shape[0]:
                entry[1] += rows
                return entry[0].at[pl.ds(entry[1] - rows, rows), :]
        raise ValueError("no room")

    r1 = wqkv.shape[0]
    jobs = {}

    def bring(name, src, target, col):
        piece = min(src.shape[0], 256)
        for n in range(0, src.shape[0], piece):
            stage = room(piece)
            copy = fetch(src.at[pl.ds(n, piece), :], stage)
            jobs.setdefault(name, []).append((copy, stage, target, col, place.y * src.shape[0] + n, piece))

    c512 = pl.ds(0, 512)
    bring("k", wqkv.at[:, pl.ds(512, 512)], Wk, 0)
    bring("v", wqkv.at[:, pl.ds(1024, 512)], Wv, 0)
    bring("q", wqkv.at[:, pl.ds(0, 512)], Wq, 0)
    tok_in = fetch(tok, xs.at[pl.ds(M, S), :])
    mem_in = fetch(mem, xs.at[pl.ds(0, M), :])
    bring("o", wo, Wo, 0)
    for c in range(FF // 512):
        bring("u", wu.at[:, pl.ds(c * 512, 512)], Wu, c * 512)
    bring("d", wd, Wd, 0)
    cot_in = fetch(cot, ct)
    bring("c", wc, Wc, 0)
    old_in = fetch(old.at[pl.ds(S // 3, old.shape[0] - S // 3), :], newold.at[pl.ds(0, old.shape[0] - S // 3), :])

    nblocks[pl.ds(place.y, 1)] = jnp.concatenate(
        [norms[...].astype(BF).astype(F32), jnp.zeros((4, norms.shape[1]), F32)], axis=0
    )[None]

    def cast(name):
        for copy, stage, target, col, start, rows in jobs[name]:
            copy.wait()
            target[rows_at(start, rows), pl.ds(col, 512)] = stage[...].astype(BF)

    cast("k")
    pl.semaphore_wait(barrier, len(partners))
    norm_sent = []
    for j in range(1, shards):
        v = nblocks.at[place.y]
        norm_sent.append(remote(v, v, (send.take(), recv.take()), place.ahead(j)))
    gathers = {}

    def launch(name, buf, split):
        gathers[name] = Gather(place, buf, send, recv, split)
        gathers[name].start()

    split = plan["split"]
    launch("k", Wk, split["k"])
    cast("v")
    launch("v", Wv, split["v"])
    cast("q")
    launch("q", Wq, split["q"])
    cast("o")
    launch("o", Wo, split["o"])
    cast("u")
    launch("u", Wu, split["u"])
    cast("d")
    launch("d", Wd, split["d"])
    cast("c")
    launch("c", Wc, split["c"])

    ids = docs[...].astype(F32)
    column = jnp.transpose(jnp.broadcast_to(ids, (8, ids.shape[1])))
    base = ids.shape[1] - L

    def see(b):
        key = column[base + 128 * b : base + 128 * b + W, 0:1]
        query = ids[:, base + T0 + 128 * b : base + T0 + 128 * b + 128]
        k = lax.broadcasted_iota(jnp.int32, (W, 128), 0)
        q = lax.broadcasted_iota(jnp.int32, (W, 128), 1) + T0
        bias[b] = jnp.where((key == query) & (k <= q), 0.0, -1e30)

    for b in range(n_q):
        see(b)
    gathers["k"].spread()
    for copy in norm_sent:
        copy.wait_recv()
    table = jnp.concatenate([nblocks[j] for j in range(shards)], axis=1)
    g1, b1, g2, b2 = table[0:1], table[1:2], table[2:3], table[3:4]

    tok_in.wait()
    mem_in.wait()

    def ln1(i, _):
        unit, _s = normalised(xs[rows_at(H0 + i * 64, 64), :].astype(F32))
        N[rows_at(i * 64, 64), :] = (unit * g1 + b1).astype(BF)
        return 0

    lax.fori_loop(0, 10, ln1, 0)
    gathers["v"].spread()
    gathers["k"].pass_on()
    lax.fori_loop(10, L // 64, ln1, 0)
    gathers["q"].spread()
    gathers["v"].pass_on()
    gathers["o"].spread()
    gathers["k"].finish()
    for c in range(2):
        cs = slice(c * 256, c * 256 + 256)
        K[:, cs] = nn(N[...], Wk[:, cs]).astype(BF)
    gathers["q"].pass_on()
    gathers["v"].finish()
    for c in range(2):
        cs = slice(c * 256, c * 256 + 256)
        V[:, cs] = nn(N[...], Wv[:, cs]).astype(BF)
    gathers["o"].pass_on()
    gathers["q"].finish()
    for c in range(2):
        cs = slice(c * 256, c * 256 + 256)
        Q[:, cs] = (nn(N[T0:, :], Wq[:, cs]).astype(BF).astype(F32) * 0.125).astype(BF)

    def attend(qb, p):
        q0, l0 = pl.multiple_of(qb * 128, 128), pl.multiple_of(p * 128, 128)
        q2 = two_heads(Q[pl.ds(q0, 128), pl.ds(l0, 128)])
        s = nt(K[pl.ds(q0, W), pl.ds(l0, 128)], q2)
        seen = bias[qb]
        s = s + jnp.concatenate([seen, seen], axis=1)
        e = jnp.exp(s - jnp.max(s, axis=0, keepdims=True))
        probs = (e * (1.0 / jnp.sum(e, axis=0, keepdims=True))).astype(BF)
        PT[p * n_q + qb] = probs
        o = tn(V[pl.ds(q0, W), pl.ds(l0, 128)], probs)
        OT[pl.ds(l0, 128), pl.ds(q0, 128)] = own_halves(o).astype(BF)

    def attend_row(i, _):
        for u in range(2):
            attend(i // 2, (i % 2) * 2 + u)
        return 0

    half = n_q
    lax.fori_loop(0, half, attend_row, 0)
    gathers["u"].spread()
    lax.fori_loop(half, 2 * n_q, attend_row, 0)
    gathers["u"].pass_on()
    gathers["o"].finish()

    for c in range(2):
        cs = slice(c * 256, c * 256 + 256)
        res[:, cs] = xs[M:, cs].astype(F32) + tn(OT[...], Wo[:, cs])

    def ln2(i, _):
        r = rows_at(i * 64, 64)
        unit, _s = normalised(res[r, :])
        lifted[r, :] = (unit * g2 + b2).astype(BF)
        return 0

    lax.fori_loop(0, S // 64, ln2, 0)
    gathers["d"].spread()
    gathers["u"].finish()
    gathers["d"].pass_on()
    gathers["d"].finish()
    cot_in.wait()

    def ffn(i, _):
        cs = rows_at(i * 256, 256, 256)
        h = nn(lifted[...], Wu[:, cs])
        ga = nt(ct[...], Wd[cs, :])
        h2 = h * h
        t = jnp.tanh(GELU_C * h * (1.0 + GELU_A * h2))
        hp = 0.5 + 0.5 * t
        act[:, cs] = (h * hp).astype(BF)
        slope = hp + (0.5 * GELU_C) * h * (1.0 - t * t) * (1.0 + (3 * GELU_A) * h2)
        gh[:, cs] = (ga * slope).astype(BF)
        return 0

    lax.fori_loop(0, FF // 256, ffn, 0)

    sums = {
        name: Total(place, gbuf[i], tbuf[i], slots[i], send, recv, plan["orders"][i]) for i, name in enumerate(GRADS)
    }
    waiting = {name: list(sums[name].steps()) for name in GRADS}
    ends = []

    def go(*names):
        for name in names:
            if waiting[name]:
                waiting[name].pop(0)()
                if not waiting[name]:
                    i = GRADS.index(name)
                    copy = pltpu.make_async_copy(tbuf[i], totals[i], local.take())
                    copy.start()
                    ends.append(copy)

    def grad_down(ref, col):
        def body(i, _):
            r = rows_at(i * 512, 512, 512)
            ref[r, :] = tn(act[:, r], ct[:, col : col + 256]).astype(BF)
            return 0

        lax.fori_loop(0, FF // 512, body, 0)

    grad_down(gbuf[0], 0)
    go("d0")
    grad_down(gbuf[1], 256)
    go("d1")
    for n in range(2):
        for c in range(2):
            gbuf[2 + n][:, c * 512 : c * 512 + 512] = tn(
                lifted[...], gh[:, n * 1024 + c * 512 : n * 1024 + c * 512 + 512]
            ).astype(BF)
        go(*(("u0", "d0") if n == 0 else ("u1", "d1")))
    for c in range(2):
        cs = slice(c * 256, c * 256 + 256)
        gl[:, cs] = nt(gh[...], Wu[cs, :])
    go("u0", "u1")

    zero = jnp.zeros((1, D), F32)

    def ln2_back(i, sums_in):
        r = rows_at(i * 64, 64)
        unit, scale = normalised(res[r, :])
        gy = gl[r, :]
        x = ct[r, :].astype(F32) + norm_back(gy, unit, scale, g2)
        gres[r, :] = x
        gr[r, :] = x.astype(BF)
        return (
            sums_in[0] + jnp.sum(gy * unit, axis=0, keepdims=True),
            sums_in[1] + jnp.sum(gy, axis=0, keepdims=True),
        )

    gain2, shift2 = lax.fori_loop(0, S // 64, ln2_back, (zero, zero))
    gbuf[4][...] = nn(OT[...], gr[...]).astype(BF)
    go("o", "d0")
    for c in range(2):
        cs = slice(c * 256, c * 256 + 256)
        dO[:, cs] = nt(gr[...], Wo[cs, :]).astype(BF)
    for c in range(2):
        cs = slice(c * 256, c * 256 + 256)
        dt = nt(Wo[cs, :], gr[...]).astype(BF).astype(F32) * OT[cs, :].astype(F32)
        for h in range(4):
            Dv[c * 4 + h : c * 4 + h + 1, :] = jnp.sum(dt[h * 64 : h * 64 + 64], axis=0, keepdims=True)
    go("o", "d0", "d1")

    def attend_back(qb, p):
        q0, l0 = pl.multiple_of(qb * 128, 128), pl.multiple_of(p * 128, 128)
        q2 = two_heads(Q[pl.ds(q0, 128), pl.ds(l0, 128)])
        do2 = two_heads(dO[pl.ds(q0, 128), pl.ds(l0, 128)])
        probs = PT[p * n_q + qb]
        dp = nt(V[pl.ds(q0, W), pl.ds(l0, 128)], do2)
        mean = jnp.concatenate([Dv[pl.ds(2 * p, 1), pl.ds(q0, 128)], Dv[pl.ds(2 * p + 1, 1), pl.ds(q0, 128)]], axis=1)
        ds = (probs.astype(F32) * (dp - mean)).astype(BF)
        dV[pl.ds(q0, W), pl.ds(l0, 128)] += nn(probs, do2)
        dK[pl.ds(q0, W), pl.ds(l0, 128)] += nn(ds, q2)
        dq = own_halves(tn(K[pl.ds(q0, W), pl.ds(l0, 128)], ds)) * 0.125
        Q[pl.ds(q0, 128), pl.ds(l0, 128)] = jnp.transpose(dq).astype(BF)

    dK[...] = jnp.zeros_like(dK)
    dV[...] = jnp.zeros_like(dV)
    for quad in range(2):
        ticks = [("d0", "d1", "u0"), ("d0", "d1", "u0"), ("d1", "u0", "u1")] if quad == 0 else [FFN + ("o",)] * 3
        for part in range(3):

            def body(qb, _):
                for u in range(2):
                    attend_back(qb, quad * 2 + u)
                return 0

            lax.fori_loop(part * n_q // 3, (part + 1) * n_q // 3, body, 0)
            go(*ticks[part])
        cs = slice(quad * 256, quad * 256 + 256)
        K[:, cs] = dK[:, cs].astype(BF)
        V[:, cs] = dV[:, cs].astype(BF)
        g = gbuf[5 + quad]
        g[:, 0:256] = tn(N[T0:, :], Q[:, cs]).astype(BF)
        g[:, 256:512] = tn(N[...], K[:, cs]).astype(BF)
        g[:, 512:768] = tn(N[...], V[:, cs]).astype(BF)
        go(*(("qa", "o") + FFN if quad == 0 else ("qb", "qa")))

    for c in range(2):
        cs = slice(c * 256, c * 256 + 256)
        dK[:, cs] = nt(K[...], Wk[cs, :]) + nt(V[...], Wv[cs, :])
        dK[T0:, cs] += nt(Q[...], Wq[cs, :])
    go(*LATE)

    def ln1_back(i, sums_in, tokens):
        unit, scale = normalised(xs[rows_at(H0 + i * 64, 64), :].astype(F32))
        gy = dK[rows_at(i * 64, 64), :]
        if tokens:
            r = rows_at(i * 64 - T0, 64)
            lifted[r, :] = (gres[r, :] + norm_back(gy, unit, scale, g1)).astype(BF)
        return (
            sums_in[0] + jnp.sum(gy * unit, axis=0, keepdims=True),
            sums_in[1] + jnp.sum(gy, axis=0, keepdims=True),
        )

    acc = lax.fori_loop(0, T0 // 64, functools.partial(ln1_back, tokens=False), (zero, zero))
    gain1, shift1 = lax.fori_loop(T0 // 64, L // 64, functools.partial(ln1_back, tokens=True), acc)
    tgrad_out = pltpu.make_async_copy(lifted, tgrad, local.take())
    tgrad_out.start()

    ngrad[0] = jnp.concatenate([gain1, shift1, gain2, shift2, jnp.zeros((4, D), F32)], axis=0)
    hops = [(place.across(bit)) for bit in place.bits]
    bit = 1
    while bit < shards:
        hops.append(place.shard_across(bit))
        bit *= 2
    norm_copies = []

    def norm_send(n):
        norm_copies.append(remote(ngrad.at[n], nslots.at[n], (send.take(), recv.take()), hops[n]))

    def norm_next(n):
        norm_copies[n].wait_recv()
        ngrad[n + 1] = ngrad[n] + nslots[n]
        if n + 1 < len(hops):
            norm_send(n + 1)

    norm_send(0)
    go(*LATE)

    for c in range(2):
        cs = slice(c * 256, c * 256 + 256)
        gr[:, cs] = (res[:, cs] + nn(act[...], Wd[:, cs])).astype(BF)
        norm_next(c)
        go(*LATE)
    out_copy = pltpu.make_async_copy(gr, out, local.take())
    out_copy.start()
    gathers["c"].spread()
    gathers["c"].pass_on()
    for n in range(D // 128):
        ev[n] = xs[pl.ds(0, S), n * 128 : n * 128 + 128].astype(F32)
    squeezed = None
    gathers["c"].finish()
    for t in range(3):
        every = [ev[n, pl.ds(t, S // 3, stride=3), :] for n in range(D // 128)]
        part = jnp.concatenate(every, axis=1).astype(BF)
        term = nn(part, Wc[t * D : (t + 1) * D, :])
        squeezed = term if squeezed is None else squeezed + term
        go(*LATE)
    dO[0 : S // 3, :] = squeezed.astype(BF)
    squeeze_copy = pltpu.make_async_copy(
        dO.at[pl.ds(0, S // 3), :], newold.at[pl.ds(old.shape[0] - S // 3, S // 3), :], local.take()
    )
    squeeze_copy.start()
    for n in range(2, len(hops)):
        norm_next(n)
        go(*LATE)
    for _ in range(20):
        go("d0", "u0", "d1", "u1", "o", "qa", "qb")
    final = ngrad[len(hops)]
    width = norms.shape[1]
    mine = final[:, 0:width]
    for j in range(1, shards):
        mine = jnp.where(place.y == j, final[:, j * width : (j + 1) * width], mine)
    norm_total[...] = mine

    for copy in ends + [tgrad_out, out_copy, squeeze_copy, old_in]:
        copy.wait()
    for name in gathers:
        gathers[name].sent()
    for name in GRADS:
        sums[name].sent()
    for copy in norm_sent + norm_copies:
        copy.wait_send()


def run_layer(sizes, tokens, memory, cmemory, docs, cotangent, wqkv, wo, wu, wd, wc, norms):
    streams, shards = sizes
    S, D = tokens.shape
    M = memory.shape[0]
    L = REACH + S
    W = REACH + 128
    FF = wu.shape[1]
    n_q = S // 128
    main, other = orders(streams, shards)
    shapes = [(FF, D // 2)] * 2 + [(D, FF // 2)] * 2 + [(D, D)] + [(D, 3 * D // 2)] * 2
    plan_orders = [main, main, main, main, main, main, main]
    slot_lists = [slot_shapes(sizes, *shapes[i], plan_orders[i]) for i in range(7)]
    hops = len(orders(streams, shards)[0]) + 1
    sems = 7 * (shards - 1) * 4 + 7 * (2 * shards + 2 * hops) + hops + shards
    plan = {
        "orders": plan_orders,
        "slot_counts": [len(s) for s in slot_lists],
        "sems": sems,
        "local": 32,
        "split": {"k": True, "v": True, "q": True, "o": True, "u": True, "d": True, "c": True},
    }
    f32, bf = (lambda *s: pltpu.VMEM(s, F32)), (lambda *s: pltpu.VMEM(s, BF))
    scratch = [
        bf(M + S, D), bf(L, D), bf(S, D), bf(L, D), bf(L, D), bf((HEADS // 2) * n_q, W, 256), bf(D, S),
        f32(n_q, W, 128), f32(S, D), f32(S, D), bf(S, D), bf(S, FF), bf(S, FF), f32(S, D), bf(S, D), bf(S, D),
        f32(HEADS, S), f32(L, D), f32(L, D), bf(S, D),
        bf(D, D), bf(D, D), bf(D, D), bf(D, D), bf(D, FF), bf(FF, D), bf(3 * D, D),
        f32(shards, 8, norms.shape[1]), f32(hops + 1, 8, D), f32(hops, 8, D), f32(D // 128, S, 128),
    ]
    scratch += [bf(*s) for s in shapes]
    scratch += [bf(s[0] // shards, s[1]) for s in shapes]
    for s in slot_lists:
        scratch += [bf(*x) for x in s]
    scratch += [pltpu.SemaphoreType.DMA((sems,)), pltpu.SemaphoreType.DMA((sems,)), pltpu.SemaphoreType.DMA((32,))]
    anywhere = pl.BlockSpec(memory_space=pl.ANY)
    vmem = pl.BlockSpec(memory_space=pltpu.VMEM)
    out_shape = [
        jax.ShapeDtypeStruct((S, D), BF),
        jax.ShapeDtypeStruct((S, D), BF),
        jax.ShapeDtypeStruct(cmemory.shape, BF),
        jax.ShapeDtypeStruct((8, norms.shape[1]), F32),
    ] + [jax.ShapeDtypeStruct((s[0] // shards, s[1]), BF) for s in shapes]
    return pl.pallas_call(
        functools.partial(layer_kernel, sizes, plan),
        out_shape=out_shape,
        in_specs=[anywhere] * 3 + [vmem] + [anywhere] * 6 + [vmem],
        out_specs=[anywhere] * 3 + [vmem] + [anywhere] * 7,
        scratch_shapes=scratch,
        compiler_params=pltpu.CompilerParams(
            collective_id=0, has_side_effects=True, vmem_limit_bytes=64 * 1024 * 1024
        ),
        name="layer",
    )(tokens, memory, cmemory, docs, cotangent, wqkv, wo, wu, wd, wc, norms)


def renew(grad, moment, average, master):
    momentum = MOMENTUM * moment + (1.0 - MOMENTUM) * grad
    updated = master - RATE * ((1.0 - MOMENTUM) * grad + MOMENTUM * momentum)
    smooth = SMOOTH * average + (1.0 - SMOOTH) * updated
    return momentum, smooth, updated


def update_kernel(steps, *refs):
    totals, masters, moments, averages = refs[0:7], refs[7:11], refs[11:15], refs[15:19]
    norm_grad, norm_old = refs[19], refs[20:23]
    passed = refs[23:27]
    grads, momenta, smooths, updates = refs[27:31], refs[31:35], refs[35:39], refs[39:43]
    norm_out = refs[43:47]
    lifted_out = refs[47]
    kept = refs[48:52]
    sems = refs[52]
    step = pl.program_id(0)
    rows = kept[1].shape[0]
    skip = passed[3].shape[0] - rows
    sources = [passed[0], passed[1], passed[2], passed[3].at[pl.ds(skip, rows), :]]
    targets = [kept[0], kept[2], kept[3], kept[1]]
    copies = [pltpu.make_async_copy(a, b, sems.at[i]) for i, (a, b) in enumerate(zip(sources, targets))]

    @pl.when(step == 0)
    def _():
        for copy in copies:
            copy.start()
        g = norm_grad[0:4, :]
        norm_out[0][...] = g
        lifted_out[...] = g[2:4]
        for ref, value in zip(norm_out[1:], renew(g, norm_old[1][...], norm_old[2][...], norm_old[0][...])):
            ref[...] = value

    d0, d1, u0, u1, o, qa, qb = [t[...].astype(F32) for t in totals]
    pieces = []
    for c in range(0, qa.shape[1], 256):
        pieces += [qa[:, c : c + 256], qb[:, c : c + 256]]
    whole = (
        jnp.concatenate(pieces, axis=1),
        o,
        jnp.concatenate([u0, u1], axis=1),
        jnp.concatenate([d0, d1], axis=1),
    )
    for i in range(4):
        grads[i][...] = whole[i]
        new = renew(whole[i], moments[i][...], averages[i][...], masters[i][...])
        momenta[i][...], smooths[i][...], updates[i][...] = new

    @pl.when(step == steps - 1)
    def _():
        for copy in copies:
            copy.wait()


def run_update(totals, masters, moments, averages, norm_grad, norm_old, output, tgrad, newold, tokens, mem_rows):
    steps = 8
    while masters[1].shape[0] % (steps * 16):
        steps //= 2

    def block(x):
        return pl.BlockSpec((x.shape[0] // steps, x.shape[1]), lambda i: (i, 0))

    def fixed(x):
        return pl.BlockSpec(x.shape, lambda i: (0, 0))

    anywhere = pl.BlockSpec(memory_space=pl.ANY)
    same = [jax.ShapeDtypeStruct(m.shape, F32) for m in masters]
    small = jax.ShapeDtypeStruct(norm_old[0].shape, F32)
    lifted = jax.ShapeDtypeStruct((2, small.shape[1]), F32)
    keep = [
        jax.ShapeDtypeStruct(output.shape, BF),
        jax.ShapeDtypeStruct((mem_rows, tokens.shape[1]), BF),
        jax.ShapeDtypeStruct(tgrad.shape, BF),
        jax.ShapeDtypeStruct(newold.shape, BF),
    ]
    passed = (output, tgrad, newold, tokens)
    return pl.pallas_call(
        functools.partial(update_kernel, steps),
        grid=(steps,),
        out_shape=same * 4 + [small] * 4 + [lifted] + keep,
        in_specs=[block(t) for t in totals]
        + [block(m) for m in masters] * 3
        + [fixed(norm_grad)]
        + [fixed(small)] * 3
        + [anywhere] * 4,
        out_specs=[block(m) for m in masters] * 4 + [fixed(small)] * 4 + [fixed(lifted)] + [anywhere] * 4,
        scratch_shapes=[pltpu.SemaphoreType.DMA((4,))],
        compiler_params=pltpu.CompilerParams(vmem_limit_bytes=48 * 1024 * 1024),
        name="update",
    )(*totals, *masters, *moments, *averages, norm_grad, *norm_old, *passed)


def on_device(
    sizes, tokens, memory, cmemory, doc_ids, cotangent,
    qkv_weight, out_weight, up_weight, down_weight, conv_weight, norm_params,
    qkv_moment, out_moment, up_moment, down_moment, norm_moment,
    qkv_average, out_average, up_average, down_average, norm_average,
):
    results = run_layer(
        sizes, tokens[0], memory[0], cmemory[0], doc_ids, cotangent[0],
        qkv_weight, out_weight, up_weight, down_weight, conv_weight, norm_params.T,
    )
    output, tgrad, newold, norm_grad = results[:4]
    new = run_update(
        results[4:],
        (qkv_weight, out_weight, up_weight, down_weight),
        (qkv_moment, out_moment, up_moment, down_moment),
        (qkv_average, out_average, up_average, down_average),
        norm_grad,
        (norm_params.T, norm_moment.T, norm_average.T),
        output, tgrad, newold, tokens[0], memory.shape[1],
    )
    grads, momenta, smooths, updates = new[0:4], new[4:8], new[8:12], new[12:16]
    norms = [x.T for x in new[16:20]]
    lifted = new[20].T
    out, new_memory, token_grad, new_cmemory = new[21:25]
    return (
        out[None], new_memory[None], new_cmemory[None], token_grad[None],
        *grads, norms[0], *momenta, norms[1], *smooths, norms[2], *updates, norms[3], lifted,
    )


def solution(mesh):
    sizes = (mesh.shape["stream"], mesh.shape["shard"])
    both = ("stream", "shard")
    wide = P(both, None, None)
    rows = P("shard", None)
    return jax.shard_map(
        functools.partial(on_device, sizes),
        mesh=mesh,
        in_specs=(wide, wide, wide, P(both, None), wide) + (rows,) * 16,
        out_specs=(wide,) * 4 + (rows,) * 21,
        check_vma=False,
    )
```

time: 637 us -> 207 us (0.32)
  waiting for transfers between devices: 263 us -> 0 us
  matrix products: 203 us -> 0 us
  Pallas kernels: 0 us -> 190 us
  blocking collectives: 54.4 us -> 0 us
  other arithmetic: 49 us -> 0 us
  local copies, waits for them, and re-layouts: 44 us -> 15.2 us
  between operations: 15.1 us -> 0.86 us
    dot_general x72 -> x0, matrix products: 203 us -> none  [the longest x16 50 us: scores_of(): jnp.einsum('qd,kd->qk', query_part, key_part, preferred_element_type=wide)]
    pallas_call x0 -> x2, Pallas kernels: none -> 190 us  [the longest x1 146 us: run_layer(): pl.pallas_call(functools.partial(layer_kernel, sizes, plan), out_shape=ou...]
    reduce_scatter x4 -> x0, waiting for transfers between devices: 129 us -> none  [the longest x1 56.7 us: on_device(): lax.psum_scatter(grad_up, 'shard', scatter_dimension=0, tiled=True)]
    psum x1 -> x0, waiting for transfers between devices: 106 us -> none  [on_device(): lax.psum((shares[0], shares[1], shares[2], shares[3], shares[4]), 'stream')]
    psum x1 -> x0, blocking collectives: 34.8 us -> none  [on_device(): lax.psum((shares[0], shares[1], shares[2], shares[3], shares[4]), 'stream')]
    all_gather x4 -> x0, waiting for transfers between devices: 28.6 us -> none  [the longest x1 22.3 us: on_device(): lax.all_gather(conv_weight.astype(narrow), 'shard', axis=0, tiled=True)]
    all_gather x2 -> x0, blocking collectives: 19.6 us -> none  [the longest x1 14.2 us: on_device(): lax.all_gather(out_weight.astype(narrow), 'shard', axis=0, tiled=True)]
    add x13 -> x0, other arithmetic: 16.2 us -> none  [the longest x5 16.1 us: renew(): smooth = SMOOTH * average + (1.0 - SMOOTH) * updated]
  transfers between devices with their start and end apart: 10 -> 0, of which waited for: 6 -> 0; matrix products, arithmetic and copies ran while one was open for 39% -> 0% of each run, Pallas kernels for 0% -> 0%
where the time goes in v1:
time: 207 us; the launch traced here: 206 us
  Pallas kernels  190 us (92%)
  local copies, waits for them, and re-layouts  15.2 us (7%)
    pallas_call x1, Pallas kernels, run_layer(): pl.pallas_call(functools.partial(layer_kernel, sizes, plan), out_shape=ou...  146 us
    pallas_call x1, Pallas kernels, run_update(): pl.pallas_call(functools.partial(update_kernel, steps), grid=(steps,), ou...  44.2 us
    unnamed x32, local copies, waits for them, and re-layouts  15.2 us

profile of v1, /device:TPU:0, one launch (start us, length us, event | category | flops | bytes accessed | tf_op | source)
XLA Modules:
  0.0 205.9 jit_solution(17108728637961972405)
XLA Ops:
  0.7 145.7 %layer.1 = (bf16[768,512]{1,0:T(8,128)(2,1)}, bf16[768,512]{1,0:T(8,128)(2,1)}, bf16[512,512]{1,0:T(8,128)(2,1)}, f32[8,256]{1,0:T(8,128)}, bf16[1024,256]{1,0:T...) custom-call(bf16[768,512]{1,0:T(8,128)(2,1)} %bitcast.20, ...), custom_call_target="tpu_custom_call" | custom-call | tf_op jit(solution)/shard_map/layer/pallas_call | solution.py:742
  146.4 0.0 copy-start
  146.4 1.0 copy-done
  147.5 0.0 copy-start.1
  147.5 1.1 copy-done.1
  148.6 0.0 copy-start.2
  148.6 1.0 copy-done.2
  149.6 0.0 copy-start.3
  149.6 1.0 copy-done.3
  150.7 0.0 copy-start.4
  150.7 1.0 copy-done.4
  151.7 0.0 copy-start.5
  151.7 1.0 copy-done.5
  152.8 0.0 copy-start.6
  152.8 1.0 copy-done.6
  153.8 0.0 copy-start.7
  153.8 1.0 copy-done.7
  154.8 0.0 copy-start.8
  154.8 1.0 copy-done.8
  155.9 0.0 copy-start.9
  155.9 1.0 copy-done.9
  156.9 0.0 copy-start.10
  156.9 1.0 copy-done.10
  157.9 0.0 copy-start.11
  157.9 0.9 copy-done.11
  158.8 0.0 copy-start.12
  158.8 0.7 copy-done.12
  159.5 0.0 copy-start.13
  159.5 0.7 copy-done.13
  160.2 0.0 copy-start.14
  160.2 0.7 copy-done.14
  160.9 0.0 copy-start.15
  160.9 0.7 copy-done.15
  161.6 44.2 %update.1 = (f32[256,1536]{1,0:T(8,128)}, f32[256,512]{1,0:T(8,128)}, f32[256,2048]{1,0:T(8,128)}, f32[1024,512]{1,0:T(8,128)}, f32[256,1536]{1,0:T(8,128)}, /*i...) custom-call(bf16[1024,256]{1,0:T(8,128)(2,1)S(1)} %copy-done.5, ...), custom_call_target="tpu_custom_call" | custom-call | tf_op jit(solution)/shard_map/update/pallas_call | solution.py:831
Async XLA Ops:
  146.4 1.0 copy-start
  147.5 1.1 copy-start.1
  148.6 1.0 copy-start.2
  149.6 1.0 copy-start.3
  150.7 1.0 copy-start.4
  151.7 1.0 copy-start.5
  152.8 1.0 copy-start.6
  153.8 1.0 copy-start.7
  154.8 1.0 copy-start.8
  155.9 1.0 copy-start.9
  156.9 1.0 copy-start.10
  157.9 0.9 copy-start.11
  158.8 0.7 copy-start.12
  159.5 0.7 copy-start.13
  160.2 0.7 copy-start.14
  160.9 0.7 copy-start.15

commit v2 on v1

v2 whole, which is shorter than its diff:
```python
import functools

import jax
import jax.numpy as jnp
from jax import lax
from jax.experimental import pallas as pl
from jax.experimental.pallas import tpu as pltpu
from jax.sharding import PartitionSpec as P

HEADS = 8
MOMENTUM = 0.9
RATE = 0.0025
SMOOTH = 0.8
REACH = 448
BF = jnp.bfloat16
F32 = jnp.float32
MESH = pl.DeviceIdType.MESH
GELU_C = 0.7978845608028654
GELU_A = 0.044715


def nn(a, b):
    return lax.dot_general(a, b, (((1,), (0,)), ((), ())), preferred_element_type=F32)


def nt(a, b):
    return lax.dot_general(a, b, (((1,), (1,)), ((), ())), preferred_element_type=F32)


def tn(a, b):
    return lax.dot_general(a, b, (((0,), (0,)), ((), ())), preferred_element_type=F32)


def normalised(x):
    center = x - jnp.mean(x, axis=-1, keepdims=True)
    scale = lax.rsqrt(jnp.mean(center * center, axis=-1, keepdims=True) + 1e-5)
    return center * scale, scale


def norm_back(grad, unit, scale, gain):
    inner = grad * gain
    first = jnp.mean(inner, axis=-1, keepdims=True)
    second = jnp.mean(inner * unit, axis=-1, keepdims=True)
    return (inner - first - unit * second) * scale


def two_heads(block):
    lane = lax.broadcasted_iota(jnp.int32, block.shape, 1)
    zero = jnp.zeros_like(block)
    low = lane < 64
    return jnp.concatenate([jnp.where(low, block, zero), jnp.where(low, zero, block)], axis=0)


def own_halves(block):
    return jnp.concatenate([block[0:64, 0:128], block[64:128, 128:256]], axis=0)


def rows_at(start, count, by=16):
    return pl.ds(pl.multiple_of(start, by), count)


class Sems:
    def __init__(self, ref, size):
        self.ref, self.size, self.used = ref, size, 0

    def take(self):
        self.used += 1
        assert self.used <= self.size
        return self.ref.at[self.used - 1]


def subsets(bits):
    found = [()]
    for bit in bits:
        found += [f + (bit,) for f in found]
    return found[1:]


class Place:
    def __init__(self, streams, shards):
        self.streams, self.shards = streams, shards
        self.s = lax.axis_index("stream")
        self.y = lax.axis_index("shard")

    def value(self, axis, bit, flipped=False):
        v = ((self.s if axis == "stream" else self.y) // bit) % 2
        return 1 - v if flipped else v

    def flip(self, bits):
        s, y = self.s, self.y
        for axis, bit in bits:
            step = bit * (1 - 2 * self.value(axis, bit))
            if axis == "stream":
                s = s + step
            else:
                y = y + step
        return s, y

    def index(self, bits, flipped=()):
        total = 0
        for axis, bit in bits:
            total = total * 2 + self.value(axis, bit, (axis, bit) in flipped)
        return total


def remote(src, dst, sems, who):
    copy = pltpu.make_async_remote_copy(
        src_ref=src, dst_ref=dst, send_sem=sems[0], recv_sem=sems[1], device_id=who, device_id_type=MESH
    )
    copy.start()
    return copy


CORE, NEAR = ("stream", 1), ("stream", 2)


class Gather:
    def __init__(self, place, buf, take, split):
        self.p, self.buf, self.take = place, buf, take
        self.rows = buf.shape[0] // place.shards
        self.split = split
        self.parts = (NEAR, CORE) if split else (CORE,)
        self.count = self.rows // 2 ** len(self.parts)
        self.deltas = subsets(shard_bits(place.shards))
        self.part = place.index(self.parts)
        self.first, self.second, self.third = [], [], []

    def view(self, owner, part):
        return self.buf.at[rows_at(owner * self.rows + part * self.count, self.count), :]

    def start(self):
        for delta in self.deltas:
            v = self.view(self.p.y, self.part)
            self.first.append(remote(v, v, self.take(), self.p.flip(delta)))

    def spread(self):
        for n, delta in enumerate(self.deltas):
            self.first[n].wait_recv()
            v = self.view(self.p.flip(delta)[1], self.part)
            if self.split:
                self.second.append(remote(v, v, self.take(), self.p.flip((NEAR,))))
            self.third.append(remote(v, v, self.take(), self.p.flip((CORE,))))

    def pass_on(self):
        if self.split:
            for n, delta in enumerate(self.deltas):
                self.second[n].wait_recv()
                v = self.view(self.p.flip(delta)[1], self.p.index(self.parts, (NEAR,)))
                self.third.append(remote(v, v, self.take(), self.p.flip((CORE,))))

    def finish(self):
        for copy in self.third:
            copy.wait_recv()

    def sent(self):
        for copy in self.first + self.second + self.third:
            copy.wait_send()


def shard_bits(shards):
    bits, bit = [], shards // 2
    while bit >= 1:
        bits.append(("shard", bit))
        bit //= 2
    return tuple(bits)


def stream_bits(streams):
    bits, bit = [], 1
    while bit < streams:
        bits.append(("stream", bit))
        bit *= 2
    return tuple(bits)


def plan_total(sizes, rows, order):
    shards = sizes[1]
    count, full, stages, shares = rows // shards, True, [], []
    for group in order:
        across = tuple(b for b in group if b[0] == "shard")
        along = tuple(b for b in group if b[0] == "stream")
        if along and count % (16 * 2 ** len(along)):
            groups = ([(across, ())] if across else []) + [((), (b,)) for b in along]
        else:
            groups = [(across, along)]
        for across, along in groups:
            scatter = count % (16 * 2 ** len(along)) == 0
            if scatter:
                count //= 2 ** len(along)
            full = full and not across
            stages.append((across + along, along if scatter else (), bool(across), shards if full else 1, count))
            if scatter and along:
                shares.insert(0, along)
    return stages, shares


class Total:
    def __init__(self, place, grad, total, slots, take, plan):
        self.p, self.grad, self.total, self.take = place, grad, total, take
        self.slots = slots
        self.stages, self.shares = plan
        self.rows = grad.shape[1]
        self.off, self.count, self.full = 0, self.rows, True
        self.live, self.done = [], []
        self.at = 0

    def begin(self):
        bits, along, across, blocks, piece = self.stages[self.at]
        slot = self.slots[self.at]
        self.live = []
        for n, delta in enumerate(subsets(bits)):
            s, y = who = self.p.flip(delta)
            rows = rows_at(self.off + self.p.index(along, delta) * piece, piece)
            if across:
                src = self.grad.at[pl.ds(y, 1), rows, :]
            elif self.full:
                src = self.grad.at[:, rows, :]
            else:
                src = self.grad.at[pl.ds(self.p.y, 1), rows, :]
            self.live.append(remote(src, slot.at[n], self.take(), who))
        self.off = self.off + self.p.index(along) * piece
        self.count = piece
        self.full = self.full and not across

    def add(self, last):
        slot = self.slots[self.at]
        rows = rows_at(self.off, self.count)
        here = slice(None) if self.full else pl.ds(self.p.y, 1)
        value = self.grad[here, rows, :].astype(F32)
        for n, copy in enumerate(self.live):
            copy.wait_recv()
            value = value + slot[n].astype(F32)
        if last:
            self.total[rows, :] = value[0].astype(BF)
        else:
            self.grad[here, rows, :] = value.astype(BF)
        self.done += self.live
        self.at += 1

    def share(self, bits):
        v = self.total.at[rows_at(self.off, self.count), :]
        self.live = [remote(v, v, self.take(), self.p.flip(delta)) for delta in subsets(bits)]
        self.off = self.off - self.p.index(bits) * self.count
        self.count *= 2 ** len(bits)

    def arrive(self):
        for copy in self.live:
            copy.wait_recv()
        self.done += self.live

    def steps(self):
        def middle():
            self.add(False)
            self.begin()

        def turn():
            self.add(True)
            self.share(self.shares[0])

        def later(bits):
            self.arrive()
            self.share(bits)

        out = [self.begin] + [middle] * (len(self.stages) - 1) + [turn]
        return out + [functools.partial(later, bits) for bits in self.shares[1:]] + [self.arrive]

    def sent(self):
        for copy in self.done:
            copy.wait_send()


class Everywhere:
    def __init__(self, place, table, slots, take, groups):
        self.p, self.table, self.slots, self.take, self.groups = place, table, slots, take, groups
        self.live, self.done, self.at = [], [], 0

    def begin(self):
        group, slot = self.groups[self.at], self.slots[self.at]
        mine = pl.ds(self.p.index(group), 1)
        slot[mine] = self.table[...][None]
        self.live = [remote(slot.at[mine], slot.at[mine], self.take(), self.p.flip(d)) for d in subsets(group)]

    def add(self):
        for copy in self.live:
            copy.wait_recv()
        self.done += self.live
        slot = self.slots[self.at]
        total = slot[0]
        for n in range(1, slot.shape[0]):
            total = total + slot[n]
        self.table[...] = total
        self.at += 1

    def steps(self):
        def middle():
            self.add()
            self.begin()

        return [self.begin] + [middle] * (len(self.groups) - 1) + [self.add]

    def sent(self):
        for copy in self.done:
            copy.wait_send()


GRADS = ("d0", "d1", "u0", "u1", "o", "qa", "qb")
WAYS = {"d0": "yxz", "d1": "yxz", "u0": "yxz", "u1": "yxz", "o": "yxz", "qa": "yxz", "qb": "yxz"}
TICKS = (
    ("d0",),
    ("d1",),
    ("d0", "u0"),
    ("d1", "u1"),
    ("u0",),
    ("u1",),
    (),
    (),
    (),
    ("d0", "o"),
    (),
    ("o",),
    (),
    (),
    ("d0",),
    ("d1",),
    (),
    ("qa",),
    (),
    ("d0", "qa"),
    ("d1", "u0"),
    (),
    (),
    (),
    ("d0", "qb"),
    ("u0", "u1"),
    ("d1", "qb"),
    (),
    ("d0", "o"),
    ("u0",),
    ("n", "d0", "u1", "qa"),
    ("d1", "o"),
    (),
    ("u0",),
    (),
    ("n", "qa", "qb"),
    ("u1",),
    ("d1",),
    ("o",),
    ("n",),
    ("d1",),
    ("qa",),
    ("u0",),
    ("u0",),
    ("qb",),
    ("u1",),
    ("o",),
    ("qa",),
    ("u1",),
    ("qb",),
    ("o",),
    ("u1",),
    ("o",),
    ("qa",),
    ("qb",),
    ("qa",),
    ("qb",),
    ("qb",),
)


def layer_kernel(
    sizes, plan, tok, mem, old, docs, cot, wqkv, wo, wu, wd, wc, norms, out, tgrad, newold, norm_total, *rest
):
    totals = rest[:7]
    (
        xs, N, Q, K, V, PT, OT, bias, res, gres, lifted, act, gh, gl, gr, dO, Dv, dK, dV, ct,
        Wq, Wk, Wv, Wo, Wu, Wd, Wc, nblocks, ngrad, ev,
    ) = rest[7:37]
    rest = rest[37:]
    gbuf, tbuf = rest[:7], rest[7:14]
    rest = rest[14:]
    slots = []
    for stages, _ in plan["totals"]:
        slots.append(rest[: len(stages)])
        rest = rest[len(stages) :]
    nslots, rest = rest[: len(plan["groups"])], rest[len(plan["groups"]) :]
    send_ref, recv_ref, local_ref = rest
    place = Place(*sizes)
    send, recv, local = Sems(send_ref, plan["sems"]), Sems(recv_ref, plan["sems"]), Sems(local_ref, plan["local"])

    def pair():
        return send.take(), recv.take()

    shards = place.shards
    S, D = tok.shape
    M = mem.shape[0]
    H0 = M - REACH
    L = REACH + S
    T0 = REACH
    W = REACH + 128
    FF = Wu.shape[1]
    n_q = S // 128

    barrier = pltpu.get_barrier_semaphore()
    for bits in plan["partners"]:
        pl.semaphore_signal(barrier, inc=1, device_id=place.flip(bits), device_id_type=MESH)

    def fetch(src, dst):
        copy = pltpu.make_async_copy(src, dst, local.take())
        copy.start()
        return copy

    pools = [dK, dV, gl, gres, res]
    free = [[ref, 0] for ref in pools]

    def room(rows):
        for entry in free:
            if entry[1] + rows <= entry[0].shape[0]:
                entry[1] += rows
                return entry[0].at[pl.ds(entry[1] - rows, rows), :]
        raise ValueError("no room")

    r1 = wqkv.shape[0]
    jobs = {}

    def bring(name, src, target, col):
        piece = min(src.shape[0], 256)
        for n in range(0, src.shape[0], piece):
            stage = room(piece)
            copy = fetch(src.at[pl.ds(n, piece), :], stage)
            jobs.setdefault(name, []).append((copy, stage, target, col, place.y * src.shape[0] + n, piece))

    c512 = pl.ds(0, 512)
    bring("k", wqkv.at[:, pl.ds(512, 512)], Wk, 0)
    bring("v", wqkv.at[:, pl.ds(1024, 512)], Wv, 0)
    bring("q", wqkv.at[:, pl.ds(0, 512)], Wq, 0)
    tok_in = fetch(tok, xs.at[pl.ds(M, S), :])
    mem_in = fetch(mem, xs.at[pl.ds(0, M), :])
    bring("o", wo, Wo, 0)
    for c in range(FF // 512):
        bring("u", wu.at[:, pl.ds(c * 512, 512)], Wu, c * 512)
    bring("d", wd, Wd, 0)
    cot_in = fetch(cot, ct)
    bring("c", wc, Wc, 0)
    old_in = fetch(old.at[pl.ds(S // 3, old.shape[0] - S // 3), :], newold.at[pl.ds(0, old.shape[0] - S // 3), :])

    nblocks[pl.ds(place.y, 1)] = jnp.concatenate(
        [norms[...].astype(BF).astype(F32), jnp.zeros((4, norms.shape[1]), F32)], axis=0
    )[None]

    def cast(name):
        for copy, stage, target, col, start, rows in jobs[name]:
            copy.wait()
            target[rows_at(start, rows), pl.ds(col, 512)] = stage[...].astype(BF)

    cast("k")
    pl.semaphore_wait(barrier, len(plan["partners"]))
    own = nblocks.at[pl.ds(place.y, 1)]
    norm_copies = [remote(own, own, pair(), place.flip(delta)) for delta in subsets(shard_bits(shards))]
    gathers = {}

    def launch(name, buf):
        gathers[name] = Gather(place, buf, pair, plan["split"][name])
        gathers[name].start()

    launch("k", Wk)
    cast("v")
    launch("v", Wv)
    cast("q")
    launch("q", Wq)
    cast("o")
    launch("o", Wo)

    ids = docs[...].astype(F32)
    column = jnp.transpose(jnp.broadcast_to(ids, (8, ids.shape[1])))
    base = ids.shape[1] - L

    def see(b):
        key = column[base + 128 * b : base + 128 * b + W, 0:1]
        query = ids[:, base + T0 + 128 * b : base + T0 + 128 * b + 128]
        k = lax.broadcasted_iota(jnp.int32, (W, 128), 0)
        q = lax.broadcasted_iota(jnp.int32, (W, 128), 1) + T0
        bias[b] = jnp.where((key == query) & (k <= q), 0.0, -1e30)

    for b in range(n_q):
        see(b)
    cast("u")
    gathers["k"].spread()
    for copy in norm_copies:
        copy.wait_recv()
    table = jnp.concatenate([nblocks[j] for j in range(shards)], axis=1)
    g1, b1, g2, b2 = table[0:1], table[1:2], table[2:3], table[3:4]

    tok_in.wait()
    mem_in.wait()

    def ln1(i, _):
        unit, _s = normalised(xs[rows_at(H0 + i * 64, 64), :].astype(F32))
        N[rows_at(i * 64, 64), :] = (unit * g1 + b1).astype(BF)
        return 0

    lax.fori_loop(0, 10, ln1, 0)
    gathers["v"].spread()
    gathers["k"].pass_on()
    launch("u", Wu)
    lax.fori_loop(10, L // 64, ln1, 0)
    gathers["q"].spread()
    gathers["v"].pass_on()
    gathers["o"].spread()
    cast("d")
    cast("c")
    gathers["k"].finish()
    for c in range(2):
        cs = slice(c * 256, c * 256 + 256)
        K[:, cs] = nn(N[...], Wk[:, cs]).astype(BF)
    gathers["q"].pass_on()
    gathers["v"].finish()
    for c in range(2):
        cs = slice(c * 256, c * 256 + 256)
        V[:, cs] = nn(N[...], Wv[:, cs]).astype(BF)
    launch("d", Wd)
    launch("c", Wc)
    gathers["o"].pass_on()
    gathers["q"].finish()
    for c in range(2):
        cs = slice(c * 256, c * 256 + 256)
        Q[:, cs] = (nn(N[T0:, :], Wq[:, cs]).astype(BF).astype(F32) * 0.125).astype(BF)

    def attend(qb, p):
        q0, l0 = pl.multiple_of(qb * 128, 128), pl.multiple_of(p * 128, 128)
        q2 = two_heads(Q[pl.ds(q0, 128), pl.ds(l0, 128)])
        s = nt(K[pl.ds(q0, W), pl.ds(l0, 128)], q2)
        seen = bias[qb]
        s = s + jnp.concatenate([seen, seen], axis=1)
        e = jnp.exp(s - jnp.max(s, axis=0, keepdims=True))
        probs = (e * (1.0 / jnp.sum(e, axis=0, keepdims=True))).astype(BF)
        PT[p * n_q + qb] = probs
        o = tn(V[pl.ds(q0, W), pl.ds(l0, 128)], probs)
        OT[pl.ds(l0, 128), pl.ds(q0, 128)] = own_halves(o).astype(BF)

    def attend_row(i, _):
        for u in range(2):
            attend(i // 2, (i % 2) * 2 + u)
        return 0

    half = n_q
    lax.fori_loop(0, half, attend_row, 0)
    gathers["u"].spread()
    lax.fori_loop(half, half + half // 2, attend_row, 0)
    gathers["u"].pass_on()
    gathers["d"].spread()
    lax.fori_loop(half + half // 2, 2 * n_q, attend_row, 0)
    gathers["d"].pass_on()
    gathers["c"].spread()
    gathers["o"].finish()

    for c in range(2):
        cs = slice(c * 256, c * 256 + 256)
        res[:, cs] = xs[M:, cs].astype(F32) + tn(OT[...], Wo[:, cs])

    def ln2(i, _):
        r = rows_at(i * 64, 64)
        unit, _s = normalised(res[r, :])
        lifted[r, :] = (unit * g2 + b2).astype(BF)
        return 0

    lax.fori_loop(0, S // 64, ln2, 0)
    gathers["c"].pass_on()
    gathers["u"].finish()
    gathers["d"].finish()
    cot_in.wait()

    def ffn(i, _):
        cs = rows_at(i * 256, 256, 256)
        h = nn(lifted[...], Wu[:, cs])
        ga = nt(ct[...], Wd[cs, :])
        h2 = h * h
        t = jnp.tanh(GELU_C * h * (1.0 + GELU_A * h2))
        hp = 0.5 + 0.5 * t
        act[:, cs] = (h * hp).astype(BF)
        slope = hp + (0.5 * GELU_C) * h * (1.0 - t * t) * (1.0 + (3 * GELU_A) * h2)
        gh[:, cs] = (ga * slope).astype(BF)
        return 0

    lax.fori_loop(0, FF // 256, ffn, 0)

    sums = {
        name: Total(place, gbuf[i], tbuf[i], slots[i], pair, plan["totals"][i]) for i, name in enumerate(GRADS)
    }
    sums["n"] = Everywhere(place, ngrad, nslots, pair, plan["groups"])
    waiting = {name: sums[name].steps() for name in sums}
    ends = []
    clock = []

    def go(names):
        for name in names:
            if not waiting[name]:
                continue
            waiting[name].pop(0)()
            if name != "n" and not waiting[name]:
                i = GRADS.index(name)
                copy = pltpu.make_async_copy(tbuf[i], totals[i], local.take())
                copy.start()
                ends.append(copy)

    def tick():
        if len(clock) < len(plan["ticks"]):
            go(plan["ticks"][len(clock)])
        clock.append(0)

    def put(ref, start, value):
        rows = value.shape[0]
        if rows > ref.shape[1]:
            n = rows // ref.shape[1]
            ref[pl.ds(start // ref.shape[1], n)] = value.astype(BF).reshape(n, ref.shape[1], value.shape[1])
        else:
            ref[start // ref.shape[1], rows_at(start % ref.shape[1], rows), :] = value.astype(BF)

    def put_all(ref, cols, value):
        ref[:, :, cols] = value.astype(BF).reshape(ref.shape[0], ref.shape[1], value.shape[1])

    def grad_down(ref, col):
        def body(i, _):
            put(ref, i * 512, tn(act[:, rows_at(i * 512, 512, 512)], ct[:, col : col + 256]))
            return 0

        lax.fori_loop(0, FF // 512, body, 0)

    for n in range(2):
        grad_down(gbuf[n], n * 256)
        tick()
    for n in range(2):
        for c in range(2):
            piece = gh[:, n * 1024 + c * 512 : n * 1024 + c * 512 + 512]
            put_all(gbuf[2 + n], slice(c * 512, c * 512 + 512), tn(lifted[...], piece))
        tick()
    for c in range(2):
        cs = slice(c * 256, c * 256 + 256)
        gl[:, cs] = nt(gh[...], Wu[cs, :])
        tick()

    zero = jnp.zeros((1, D), F32)

    def ln2_back(i, sums_in):
        r = rows_at(i * 64, 64)
        unit, scale = normalised(res[r, :])
        gy = gl[r, :]
        x = ct[r, :].astype(F32) + norm_back(gy, unit, scale, g2)
        gres[r, :] = x
        gr[r, :] = x.astype(BF)
        return (
            sums_in[0] + jnp.sum(gy * unit, axis=0, keepdims=True),
            sums_in[1] + jnp.sum(gy, axis=0, keepdims=True),
        )

    second = (zero, zero)
    for n in range(3):
        second = lax.fori_loop(n * S // 192, (n + 1) * S // 192, ln2_back, second)
        tick()
    put_all(gbuf[4], slice(0, D), nn(OT[...], gr[...]))
    tick()
    for c in range(2):
        cs = slice(c * 256, c * 256 + 256)
        dO[:, cs] = nt(gr[...], Wo[cs, :]).astype(BF)
    for c in range(2):
        cs = slice(c * 256, c * 256 + 256)
        dt = nt(Wo[cs, :], gr[...]).astype(BF).astype(F32) * OT[cs, :].astype(F32)
        for h in range(4):
            Dv[c * 4 + h : c * 4 + h + 1, :] = jnp.sum(dt[h * 64 : h * 64 + 64], axis=0, keepdims=True)
    dK[...] = jnp.zeros_like(dK)
    dV[...] = jnp.zeros_like(dV)
    tick()

    def attend_back(qb, p):
        q0, l0 = pl.multiple_of(qb * 128, 128), pl.multiple_of(p * 128, 128)
        q2 = two_heads(Q[pl.ds(q0, 128), pl.ds(l0, 128)])
        do2 = two_heads(dO[pl.ds(q0, 128), pl.ds(l0, 128)])
        probs = PT[p * n_q + qb]
        dp = nt(V[pl.ds(q0, W), pl.ds(l0, 128)], do2)
        mean = jnp.concatenate([Dv[pl.ds(2 * p, 1), pl.ds(q0, 128)], Dv[pl.ds(2 * p + 1, 1), pl.ds(q0, 128)]], axis=1)
        ds = (probs.astype(F32) * (dp - mean)).astype(BF)
        dV[pl.ds(q0, W), pl.ds(l0, 128)] += nn(probs, do2)
        dK[pl.ds(q0, W), pl.ds(l0, 128)] += nn(ds, q2)
        dq = own_halves(tn(K[pl.ds(q0, W), pl.ds(l0, 128)], ds)) * 0.125
        Q[pl.ds(q0, 128), pl.ds(l0, 128)] = jnp.transpose(dq).astype(BF)

    for quad in range(2):
        for qb in range(n_q):
            for u in range(2):
                attend_back(qb, quad * 2 + u)
            tick()
        cs = slice(quad * 256, quad * 256 + 256)
        K[:, cs] = dK[:, cs].astype(BF)
        V[:, cs] = dV[:, cs].astype(BF)
        g = gbuf[5 + quad]
        put_all(g, slice(0, 256), tn(N[T0:, :], Q[:, cs]))
        put_all(g, slice(256, 512), tn(N[...], K[:, cs]))
        put_all(g, slice(512, 768), tn(N[...], V[:, cs]))
        tick()

    for c in range(2):
        cs = slice(c * 256, c * 256 + 256)
        dK[:, cs] = nt(K[...], Wk[cs, :]) + nt(V[...], Wv[cs, :])
        dK[T0:, cs] += nt(Q[...], Wq[cs, :])
        tick()

    def ln1_back(i, sums_in, tokens):
        unit, scale = normalised(xs[rows_at(H0 + i * 64, 64), :].astype(F32))
        gy = dK[rows_at(i * 64, 64), :]
        if tokens:
            r = rows_at(i * 64 - T0, 64)
            lifted[r, :] = (gres[r, :] + norm_back(gy, unit, scale, g1)).astype(BF)
        return (
            sums_in[0] + jnp.sum(gy * unit, axis=0, keepdims=True),
            sums_in[1] + jnp.sum(gy, axis=0, keepdims=True),
        )

    first = lax.fori_loop(0, T0 // 64, functools.partial(ln1_back, tokens=False), (zero, zero))
    tick()
    for n in range(3):
        low, high = (T0 + n * S // 3) // 64, (T0 + (n + 1) * S // 3) // 64
        first = lax.fori_loop(low, high, functools.partial(ln1_back, tokens=True), first)
        if n == 2:
            ngrad[...] = jnp.concatenate([*first, *second, jnp.zeros((4, D), F32)], axis=0)
        tick()
    tgrad_out = pltpu.make_async_copy(lifted, tgrad, local.take())
    tgrad_out.start()

    for c in range(2):
        cs = slice(c * 256, c * 256 + 256)
        gr[:, cs] = (res[:, cs] + nn(act[...], Wd[:, cs])).astype(BF)
        tick()
    out_copy = pltpu.make_async_copy(gr, out, local.take())
    out_copy.start()
    for n in range(D // 128):
        ev[n] = xs[pl.ds(0, S), n * 128 : n * 128 + 128].astype(F32)
    squeezed = None
    gathers["c"].finish()
    for t in range(3):
        every = [ev[n, pl.ds(t, S // 3, stride=3), :] for n in range(D // 128)]
        part = jnp.concatenate(every, axis=1).astype(BF)
        term = nn(part, Wc[t * D : (t + 1) * D, :])
        squeezed = term if squeezed is None else squeezed + term
        tick()
    dO[0 : S // 3, :] = squeezed.astype(BF)
    squeeze_copy = pltpu.make_async_copy(
        dO.at[pl.ds(0, S // 3), :], newold.at[pl.ds(old.shape[0] - S // 3, S // 3), :], local.take()
    )
    squeeze_copy.start()
    while len(clock) < len(plan["ticks"]):
        tick()
    while any(waiting.values()):
        go([name for name in waiting if waiting[name]])
    final = ngrad[...]
    width = norms.shape[1]
    mine = final[:, 0:width]
    for j in range(1, shards):
        mine = jnp.where(place.y == j, final[:, j * width : (j + 1) * width], mine)
    norm_total[...] = mine

    for copy in ends + [tgrad_out, out_copy, squeeze_copy, old_in]:
        copy.wait()
    for part in list(gathers.values()) + list(sums.values()):
        part.sent()
    for copy in norm_copies:
        copy.wait_send()


def run_layer(sizes, tokens, memory, cmemory, docs, cotangent, wqkv, wo, wu, wd, wc, norms):
    streams, shards = sizes
    S, D = tokens.shape
    M = memory.shape[0]
    L = REACH + S
    W = REACH + 128
    FF = wu.shape[1]
    n_q = S // 128
    shapes = [(FF, D // 2)] * 2 + [(D, FF // 2)] * 2 + [(D, D)] + [(D, 3 * D // 2)] * 2
    shapes = [(shards, rows // shards, cols) for rows, cols in shapes]
    across, along = shard_bits(shards), stream_bits(streams)
    far = [along[i : i + 2] for i in range(2, len(along), 2)]
    ways = {
        "yxz": [(CORE,), across, (NEAR,)] + far,
        "xyz": [(CORE,), (NEAR,), across] + far,
        "xzy": [(CORE,), (NEAR,)] + far + [across],
        "yx.z": [(CORE,), across + (NEAR,)] + far,
    }
    totals = [plan_total(sizes, FF if i < 2 else D, ways[WAYS[name]]) for i, name in enumerate(GRADS)]
    groups = [across + (NEAR, CORE)] + far
    used = [subsets(across), subsets((NEAR, CORE))] + [subsets(g) for g in groups]
    for stages, shares in totals:
        used += [subsets(stage[0]) for stage in stages] + [subsets(bits) for bits in shares]
    partners = sorted({tuple(sorted(delta)) for some in used for delta in some})
    sems = 7 * 4 * (shards - 1) + len(subsets(across)) + sum(len(subsets(g)) for g in groups)
    for stages, shares in totals:
        sems += sum(len(subsets(stage[0])) for stage in stages) + sum(len(subsets(bits)) for bits in shares)
    plan = {
        "totals": totals,
        "groups": groups,
        "partners": partners,
        "ticks": TICKS,
        "sems": sems,
        "local": 32,
        "split": {"k": True, "v": True, "q": True, "o": True, "u": True, "d": True, "c": True},
    }
    f32, bf = (lambda *s: pltpu.VMEM(s, F32)), (lambda *s: pltpu.VMEM(s, BF))
    scratch = [
        bf(M + S, D), bf(L, D), bf(S, D), bf(L, D), bf(L, D), bf((HEADS // 2) * n_q, W, 256), bf(D, S),
        f32(n_q, W, 128), f32(S, D), f32(S, D), bf(S, D), bf(S, FF), bf(S, FF), f32(S, D), bf(S, D), bf(S, D),
        f32(HEADS, S), f32(L, D), f32(L, D), bf(S, D),
        bf(D, D), bf(D, D), bf(D, D), bf(D, D), bf(D, FF), bf(FF, D), bf(3 * D, D),
        f32(shards, 8, norms.shape[1]), f32(8, D), f32(D // 128, S, 128),
    ]
    scratch += [bf(*s) for s in shapes]
    scratch += [bf(s[1], s[2]) for s in shapes]
    for (stages, _), s in zip(totals, shapes):
        scratch += [bf(len(subsets(bits)), blocks, piece, s[2]) for bits, _b, _a, blocks, piece in stages]
    scratch += [f32(2 ** len(g), 8, D) for g in groups]
    scratch += [pltpu.SemaphoreType.DMA((sems,)), pltpu.SemaphoreType.DMA((sems,)), pltpu.SemaphoreType.DMA((32,))]
    anywhere = pl.BlockSpec(memory_space=pl.ANY)
    vmem = pl.BlockSpec(memory_space=pltpu.VMEM)
    out_shape = [
        jax.ShapeDtypeStruct((S, D), BF),
        jax.ShapeDtypeStruct((S, D), BF),
        jax.ShapeDtypeStruct(cmemory.shape, BF),
        jax.ShapeDtypeStruct((8, norms.shape[1]), F32),
    ] + [jax.ShapeDtypeStruct((s[1], s[2]), BF) for s in shapes]
    return pl.pallas_call(
        functools.partial(layer_kernel, sizes, plan),
        out_shape=out_shape,
        in_specs=[anywhere] * 3 + [vmem] + [anywhere] * 6 + [vmem],
        out_specs=[anywhere] * 3 + [vmem] + [anywhere] * 7,
        scratch_shapes=scratch,
        compiler_params=pltpu.CompilerParams(
            collective_id=0, has_side_effects=True, vmem_limit_bytes=64 * 1024 * 1024
        ),
        name="layer",
    )(tokens, memory, cmemory, docs, cotangent, wqkv, wo, wu, wd, wc, norms)


def renew(grad, moment, average, master):
    momentum = MOMENTUM * moment + (1.0 - MOMENTUM) * grad
    updated = master - RATE * ((1.0 - MOMENTUM) * grad + MOMENTUM * momentum)
    smooth = SMOOTH * average + (1.0 - SMOOTH) * updated
    return momentum, smooth, updated


def update_kernel(*refs):
    totals, masters, moments, averages = refs[0:7], refs[7:11], refs[11:15], refs[15:19]
    norm_grad, norm_old = refs[19], refs[20:23]
    passed = refs[23:27]
    grads, momenta, smooths, updates = refs[27:31], refs[31:35], refs[35:39], refs[39:43]
    norm_out = refs[43:47]
    lifted_out = refs[47]
    kept = refs[48:52]
    step = pl.program_id(0)
    for source, target in zip(passed, kept):
        target[...] = source[...]

    @pl.when(step == 0)
    def _():
        g = norm_grad[0:4, :]
        norm_out[0][...] = g
        lifted_out[...] = g[2:4]
        for ref, value in zip(norm_out[1:], renew(g, norm_old[1][...], norm_old[2][...], norm_old[0][...])):
            ref[...] = value

    d0, d1, u0, u1, o, qa, qb = [t[...].astype(F32) for t in totals]
    pieces = []
    for c in range(0, qa.shape[1], 256):
        pieces += [qa[:, c : c + 256], qb[:, c : c + 256]]
    whole = (
        jnp.concatenate(pieces, axis=1),
        o,
        jnp.concatenate([u0, u1], axis=1),
        jnp.concatenate([d0, d1], axis=1),
    )
    for i in range(4):
        grads[i][...] = whole[i]
        new = renew(whole[i], moments[i][...], averages[i][...], masters[i][...])
        momenta[i][...], smooths[i][...], updates[i][...] = new


def run_update(totals, masters, moments, averages, norm_grad, norm_old, output, tgrad, newold, tokens, mem_rows):
    steps = 8
    while masters[1].shape[0] % (steps * 16):
        steps //= 2

    def block(x):
        return pl.BlockSpec((x.shape[0] // steps, x.shape[1]), lambda i: (i, 0))

    def fixed(x):
        return pl.BlockSpec(x.shape, lambda i: (0, 0))

    skip = (tokens.shape[0] - mem_rows) // (mem_rows // steps)
    recent = pl.BlockSpec((mem_rows // steps, tokens.shape[1]), lambda i: (i + skip, 0))
    same = [jax.ShapeDtypeStruct(m.shape, F32) for m in masters]
    small = jax.ShapeDtypeStruct(norm_old[0].shape, F32)
    lifted = jax.ShapeDtypeStruct((2, small.shape[1]), F32)
    keep = [
        jax.ShapeDtypeStruct(output.shape, BF),
        jax.ShapeDtypeStruct(tgrad.shape, BF),
        jax.ShapeDtypeStruct(newold.shape, BF),
        jax.ShapeDtypeStruct((mem_rows, tokens.shape[1]), BF),
    ]
    passed = (output, tgrad, newold, tokens)
    return pl.pallas_call(
        update_kernel,
        grid=(steps,),
        out_shape=same * 4 + [small] * 4 + [lifted] + keep,
        in_specs=[block(t) for t in totals]
        + [block(m) for m in masters] * 3
        + [fixed(norm_grad)]
        + [fixed(small)] * 3
        + [block(x) for x in passed[:3]]
        + [recent],
        out_specs=[block(m) for m in masters] * 4 + [fixed(small)] * 4 + [fixed(lifted)] + [block(x) for x in keep],
        compiler_params=pltpu.CompilerParams(vmem_limit_bytes=64 * 1024 * 1024),
        name="update",
    )(*totals, *masters, *moments, *averages, norm_grad, *norm_old, *passed)


def on_device(
    sizes, tokens, memory, cmemory, doc_ids, cotangent,
    qkv_weight, out_weight, up_weight, down_weight, conv_weight, norm_params,
    qkv_moment, out_moment, up_moment, down_moment, norm_moment,
    qkv_average, out_average, up_average, down_average, norm_average,
):
    results = run_layer(
        sizes, tokens[0], memory[0], cmemory[0], doc_ids, cotangent[0],
        qkv_weight, out_weight, up_weight, down_weight, conv_weight, norm_params.T,
    )
    output, tgrad, newold, norm_grad = results[:4]
    new = run_update(
        results[4:],
        (qkv_weight, out_weight, up_weight, down_weight),
        (qkv_moment, out_moment, up_moment, down_moment),
        (qkv_average, out_average, up_average, down_average),
        norm_grad,
        (norm_params.T, norm_moment.T, norm_average.T),
        output, tgrad, newold, tokens[0], memory.shape[1],
    )
    grads, momenta, smooths, updates = new[0:4], new[4:8], new[8:12], new[12:16]
    norms = [x.T for x in new[16:20]]
    lifted = new[20].T
    out, token_grad, new_cmemory, new_memory = new[21:25]
    return (
        out[None], new_memory[None], new_cmemory[None], token_grad[None],
        *grads, norms[0], *momenta, norms[1], *smooths, norms[2], *updates, norms[3], lifted,
    )


def solution(mesh):
    sizes = (mesh.shape["stream"], mesh.shape["shard"])
    both = ("stream", "shard")
    wide = P(both, None, None)
    rows = P("shard", None)
    return jax.shard_map(
        functools.partial(on_device, sizes),
        mesh=mesh,
        in_specs=(wide, wide, wide, P(both, None), wide) + (rows,) * 16,
        out_specs=(wide,) * 4 + (rows,) * 21,
        check_vma=False,
    )
```

time: 207 us -> 147 us (0.71)
  Pallas kernels: 190 us -> 145 us
  local copies, waits for them, and re-layouts: 15.2 us -> 0 us
    pallas_call x1, Pallas kernels: 44.2 us -> 18.9 us  [run_update(): pl.pallas_call(update_kernel, grid=(steps,), out_shape=same * 4 + [small]...]
    pallas_call x1, Pallas kernels: 146 us -> 126 us  [run_layer(): pl.pallas_call(functools.partial(layer_kernel, sizes, plan), out_shape=ou...]
    unnamed x32 -> x0, local copies, waits for them, and re-layouts: 15.2 us -> none
where the time goes in v2:
time: 147 us; the launch traced here: 145 us
  Pallas kernels  145 us (99%)
    pallas_call x1, Pallas kernels, run_layer(): pl.pallas_call(functools.partial(layer_kernel, sizes, plan), out_shape=ou...  126 us
    pallas_call x1, Pallas kernels, run_update(): pl.pallas_call(update_kernel, grid=(steps,), out_shape=same * 4 + [small]...  18.9 us

profile of v2, /device:TPU:0, one launch (start us, length us, event | category | flops | bytes accessed | tf_op | source)
XLA Modules:
  0.0 145.4 jit_solution(1481975413379393734)
XLA Ops:
  0.7 125.6 %layer.1 = (bf16[768,512]{1,0:T(8,128)(2,1)}, bf16[768,512]{1,0:T(8,128)(2,1)}, bf16[512,512]{1,0:T(8,128)(2,1)}, f32[8,256]{1,0:T(8,128)}, bf16[1024,256]{1,0:T...) custom-call(bf16[768,512]{1,0:T(8,128)(2,1)} %bitcast.16, ...), custom_call_target="tpu_custom_call" | custom-call | tf_op jit(solution)/shard_map/layer/pallas_call | solution.py:826
  126.3 18.9 %update.1 = (f32[256,1536]{1,0:T(8,128)}, f32[256,512]{1,0:T(8,128)}, f32[256,2048]{1,0:T(8,128)}, f32[1024,512]{1,0:T(8,128)}, f32[256,1536]{1,0:T(8,128)}, /*i...) custom-call(bf16[1024,256]{1,0:T(8,128)(2,1)} %get-tuple-element.61., ...), custom_call_target="tpu_custom_call" | custom-call | tf_op jit(solution)/shard_map/update/pallas_call | solution.py:905
